TPU v7x, 256 devices: a whole 4x4x8 slice. The times are simulated.
256 devices in a mesh: kv: 8 (over y, x_hi), ctx: 32 (over z, x_lo, core).
Axes of the slice: x: 4 (x_hi: 2, x_lo: 2; x = x_hi * 2 + x_lo), y: 4, z: 8, core: 2. Of those that a mesh axis runs over, the one named last changes fastest.
Arguments:
- queries: bfloat16 [8192, 64, 128], P(('ctx', 'kv')), may hold values from -9 to 9
- keys: bfloat16 [8192, 8, 128], P(('ctx', 'kv')), may hold values from -5 to 5
- values: bfloat16 [8192, 8, 128], P(('ctx', 'kv')), may hold values from -6 to 6
- offsets: int32 [8192, 8, 128], P(('ctx', 'kv')), may hold values from 0 to 255
- smooth_exp: int32 [8, 128], replicated, may hold values from -1 to 1
- scale_exp: int32 [8, 128], replicated, may hold values from -6 to -5
- placement: int32 [8192], replicated, may hold values from 0 to 8191, as said below
- doc_lengths: int32 [16], replicated, may hold values from 1 to 2048, 8192 in all
Outputs:
- attended: bfloat16 [8192, 64, 128], P(('ctx', 'kv'))
Inputs may be any that keep to these rules, and one draw needn't show every extreme that they name: `placement`: each aligned run of 32 entries holds 32 consecutive positions starting at a multiple of 32; every position appears once.
All inputs are finite; a program needn't handle non-finite values.
Results may differ from a plain program's by a relative error of at most 0.008.
Values may be sent and summed in bfloat16 or wider, within the bound.
A program may use at most 64 MiB of HBM per device.

v0:
```python
import jax
import jax.numpy as jnp
from jax import lax
from jax.sharding import PartitionSpec as P


def quant_keys(keys, smooth_exp, scale_exp, offsets):
    shift_all = jnp.left_shift(jnp.int32(1), -(smooth_exp + scale_exp)).astype(jnp.float32)
    key_codes = jnp.floor(
        keys.astype(jnp.float32) * shift_all + offsets.astype(jnp.float32) / 256.0
    )
    key_codes = jnp.clip(key_codes, -128.0, 127.0)
    shift_back = jnp.left_shift(jnp.int32(1), -scale_exp).astype(jnp.float32)
    return (key_codes / shift_back).astype(jnp.bfloat16)


def scale_queries(queries, smooth_exp):
    lifted = jnp.left_shift(jnp.int32(1), smooth_exp + 1).astype(jnp.float32) * 0.5
    group = queries.shape[1] // smooth_exp.shape[0]
    lifted = jnp.repeat(lifted, group, axis=0)
    return (queries.astype(jnp.float32) * lifted).astype(jnp.bfloat16)


def doc_of(positions, doc_lengths):
    doc_ends = jnp.cumsum(doc_lengths)
    return jnp.sum((positions[:, None] >= doc_ends[None, :]).astype(jnp.int32), axis=1)


def merge_block(running, grouped, allowed, key_block, value_block):
    factor = grouped.shape[-1] ** (-0.5)
    running_max, running_sum, running_out = running
    scores = (
        jnp.einsum("qhgd,khd->hgqk", grouped, key_block, preferred_element_type=jnp.float32)
        * factor
    )
    scores = jnp.where(allowed[None, None], scores, -1e30)
    new_max = jnp.maximum(running_max, jnp.max(scores, axis=-1))
    weights = jnp.where(allowed[None, None], jnp.exp(scores - new_max[..., None]), 0.0).astype(
        jnp.bfloat16
    )
    shrink = jnp.exp(running_max - new_max)
    new_sum = running_sum * shrink + jnp.sum(weights.astype(jnp.float32), axis=-1)
    new_out = running_out * shrink[..., None] + jnp.einsum(
        "hgqk,khd->hgqd", weights, value_block, preferred_element_type=jnp.float32
    )
    return (new_max, new_sum, new_out)


def accumulate(carried, grouped, pos_query, doc_query, key_block, value_block, pos_key, doc_key):
    allowed = (pos_key[None, :] <= pos_query[:, None]) & (doc_key[None, :] == doc_query[:, None])
    return merge_block(carried, grouped, allowed, key_block, value_block)


def pick_rows(piece_rows, tok_rows):
    ceiling = min(piece_rows, max(1024, tok_rows))
    for block_rows in range(ceiling, 0, -1):
        if piece_rows % block_rows == 0:
            return block_rows
    return piece_rows


def shards(queries, keys, values, offsets, smooth_exp, scale_exp, placement, doc_lengths):
    scaled = scale_queries(queries, smooth_exp)
    coded = quant_keys(keys, smooth_exp, scale_exp, offsets)
    my_queries, my_keys, my_values = (
        lax.all_to_all(scaled, "kv", split_axis=1, concat_axis=0, tiled=True),
        lax.all_to_all(coded, "kv", split_axis=1, concat_axis=0, tiled=True),
        lax.all_to_all(values, "kv", split_axis=1, concat_axis=0, tiled=True),
    )
    tok_rows = my_queries.shape[0]
    kv_local = my_keys.shape[1]
    group = my_queries.shape[1] // kv_local
    head_dim = my_queries.shape[2]
    grouped = my_queries.reshape(tok_rows, kv_local, group, head_dim)
    my_index = lax.axis_index("ctx")
    pos_query = lax.dynamic_slice_in_dim(placement, my_index * tok_rows, tok_rows, 0)
    doc_query = doc_of(pos_query, doc_lengths)
    start_max = jnp.full((kv_local, group, tok_rows), -1e30, jnp.float32)
    start_sum = jnp.zeros((kv_local, group, tok_rows), jnp.float32)
    start_out = jnp.zeros((kv_local, group, tok_rows, head_dim), jnp.float32)
    piece_keys = lax.all_gather(my_keys, "ctx", axis=0, tiled=True)
    piece_values = lax.all_gather(my_values, "ctx", axis=0, tiled=True)
    piece_rows = piece_keys.shape[0]
    doc_piece = doc_of(placement, doc_lengths)
    block_rows = pick_rows(piece_rows, tok_rows)

    def advance(i, running):
        offset = (i * block_rows).astype(jnp.int32)
        key_block = lax.dynamic_slice_in_dim(piece_keys, offset, block_rows, 0)
        value_block = lax.dynamic_slice_in_dim(piece_values, offset, block_rows, 0)
        pos_key = lax.dynamic_slice_in_dim(placement, offset, block_rows, 0)
        doc_key = lax.dynamic_slice_in_dim(doc_piece, offset, block_rows, 0)
        return accumulate(
            running, grouped, pos_query, doc_query, key_block, value_block, pos_key, doc_key
        )

    final_max, final_sum, final_out = lax.fori_loop(
        0, piece_rows // block_rows, advance, (start_max, start_sum, start_out)
    )
    result = (final_out / final_sum[..., None]).astype(jnp.bfloat16)
    result = jnp.transpose(result, (2, 0, 1, 3)).reshape(tok_rows, kv_local * group, head_dim)
    return lax.all_to_all(result, "kv", split_axis=0, concat_axis=1, tiled=True)


def solution(mesh):
    in_specs = (
        P(("ctx", "kv"), None, None),
        P(("ctx", "kv"), None, None),
        P(("ctx", "kv"), None, None),
        P(("ctx", "kv"), None, None),
        P(),
        P(),
        P(),
        P(),
    )
    out_specs = P(("ctx", "kv"), None, None)
    return jax.shard_map(shards, mesh=mesh, in_specs=in_specs, out_specs=out_specs, check_vma=False)
```

profile of v0, /device:TPU:1, one launch (start us, length us, event | category | flops | bytes accessed | tf_op | source)
XLA Modules:
  0.0 296.4 jit_solution(1370715441567637344)
XLA Ops:
  8.2 14.1 %all_to_all.69 = bf16[32,8,128]{2,0,1:T(8,128)(2,1)} all-to-all(bf16[32,8,128]{2,0,1:T(8,128)(2,1)S(1)} %fusion.25), channel_id=1, replica_groups=mesh['kv'=8,'ctx'=32] {'kv'}, dimensions={1} | all-to-all | bytes 131072 | tf_op jit(solution)/shard_map/all_to_all | solution.py:67
  23.2 9.8 %all_to_all.70 = bf16[32,8,128]{2,0,1:T(8,128)(2,1)} all-to-all(bf16[32,8,128]{2,0,1:T(8,128)(2,1)S(1)} %copy.37), channel_id=1, replica_groups=mesh['kv'=8,'ctx'=32] {'kv'}, dimensions={1} | all-to-all | bytes 131072 | tf_op jit(solution)/shard_map/all_to_all | solution.py:68
  36.0 3.5 %all-to-all-start.1 = ((bf16[32,64,128]{2,0,1:T(8,128)(2,1)}), bf16[32,64,128]{2,0,1:T(8,128)(2,1)S(1)}, u32[]{:S(2)}, u32[]{:S(2)}) async-start(bf16[32,64,128]{2,0,1:T(8,128)(2,1)} %multiply_convert_fusion), calls=%async_computation.1 | async-start | bytes 1048576 | tf_op jit(solution)/shard_map/all_to_all | solution.py:66
  42.2 7.2 %all-to-all-done.1 = bf16[32,64,128]{2,0,1:T(8,128)(2,1)S(1)} async-done(((bf16[32,64,128]{2,0,1:T(8,128)(2,1)}), bf16[32,64,128]{2,0,1:T(8,128)(2,1)S(1)}, u32[]{:S(2)}, u32[]{:S(2)}) %all-to-all-start.1) | async-done | bytes 524320 | tf_op jit(solution)/shard_map/all_to_all | solution.py:66
  49.5 38.2 %all-gather.3.cloned.1.call-done = bf16[8192,1,128]{2,0,1:T(8,128)(2,1)} async-done(((bf16[256,1,128]{2,0,1:T(8,128)(2,1)}), bf16[8192,1,128]{2,0,1:T(8,128)(2,1)}) %all-gather.3.cloned.1.call-update) | async-done | bytes 2097168 | tf_op jit(solution)/shard_map/all_gather | solution.py:81
  87.7 66.2 %all-gather.5.cloned.1.call-done = bf16[8192,1,128]{2,0,1:T(8,128)(2,1)} async-done(((bf16[256,1,128]{2,0,1:T(8,128)(2,1)}), bf16[8192,1,128]{2,0,1:T(8,128)(2,1)}) %all-gather.5.cloned.1.call-update) | async-done | bytes 2097168 | tf_op jit(solution)/shard_map/all_gather | solution.py:82
  153.9 117.1 %while.18 = (s32[]{:T(128)}, f32[1,8,256]{2,1,0:T(8,128)S(1)}, f32[1,8,256]{2,1,0:T(8,128)S(1)}, f32[1,8,256,128]{3,2,1,0:T(8,128)S(1)}, s32[8192]{0:T(1024)}, /...) while((s32[]{:T(128)}, f32[1,8,256]{2,1,0:T(8,128)S(1)}, ...), condition=%wide.region_6.7_spmd.clone, body=%wide.region_3.6_spmd.clone.sunk | while | flops 1106784256 | bytes 63072496 | solution.py:97
  154.9 5.6 %fusion.33 = (f32[8,256]{1,0:T(8,128)S(1)}, f32[1024,256,8]{1,0,2:T(8,128)}) fusion(pred[256,1024]{0,1:T(8,128)(4,1)S(1)} %compare_and_fusion.2, bf16[256,1,8,128]{3,0,2,1:T(8,128)(2,1)S(1)} %get-tuple-element.370, bf16[8192,1,128]{2,0,1:T(8,128)(2,1)} %get-tuple-element.369, s32[]{:T(128)S(6)} %select_n.59), kind=kOutput, calls=%fused_computation.3.clone.1 | convolution fusion | flops 543160320 | bytes 9445380 | tf_op jit(solution)/shard_map/while/body/eval_jaxpr/qhgd,khd->hgqk/dot_general | solution.py:33
  160.6 5.0 %fusion.35 = f32[1,8,256,128]{3,2,1,0:T(8,128)S(1)} fusion(f32[1,8,256,128]{3,2,1,0:T(8,128)S(1)} %get-tuple-element.349, f32[8,256]{1,0:T(8,128)S(1)} %get-tuple-element.330, pred[]{:T(512)S(6)} %compare.3, bf16[8192,1,128]{2,0,1:T(8,128)(2,1)} %get-tuple-element.371, s32[]{:T(128)S(6)} %select_n.59, f32[1024,256,8]{1,0,2:T(8,128)} %get-tuple-element.329, ...), kind=kOutput, calls=%fused_computation.7.clone.1 | convolution fusion | flops 548143104 | bytes 11026437 | tf_op jit(solution)/shard_map/while/body/eval_jaxpr/hgqk,khd->hgqd/dot_general | solution.py:43
  169.6 5.6 %fusion.33 = (f32[8,256]{1,0:T(8,128)S(1)}, f32[1024,256,8]{1,0,2:T(8,128)}) fusion(pred[256,1024]{0,1:T(8,128)(4,1)S(1)} %compare_and_fusion.2, bf16[256,1,8,128]{3,0,2,1:T(8,128)(2,1)S(1)} %get-tuple-element.370, bf16[8192,1,128]{2,0,1:T(8,128)(2,1)} %get-tuple-element.369, s32[]{:T(128)S(6)} %select_n.59), kind=kOutput, calls=%fused_computation.3.clone.1 | convolution fusion | flops 543160320 | bytes 9445380 | tf_op jit(solution)/shard_map/while/body/eval_jaxpr/qhgd,khd->hgqk/dot_general | solution.py:33
  175.2 5.0 %fusion.35 = f32[1,8,256,128]{3,2,1,0:T(8,128)S(1)} fusion(f32[1,8,256,128]{3,2,1,0:T(8,128)S(1)} %get-tuple-element.349, f32[8,256]{1,0:T(8,128)S(1)} %get-tuple-element.330, pred[]{:T(512)S(6)} %compare.3, bf16[8192,1,128]{2,0,1:T(8,128)(2,1)} %get-tuple-element.371, s32[]{:T(128)S(6)} %select_n.59, f32[1024,256,8]{1,0,2:T(8,128)} %get-tuple-element.329, ...), kind=kOutput, calls=%fused_computation.7.clone.1 | convolution fusion | flops 548143104 | bytes 11026437 | tf_op jit(solution)/shard_map/while/body/eval_jaxpr/hgqk,khd->hgqd/dot_general | solution.py:43
  184.2 5.6 %fusion.33 = (f32[8,256]{1,0:T(8,128)S(1)}, f32[1024,256,8]{1,0,2:T(8,128)}) fusion(pred[256,1024]{0,1:T(8,128)(4,1)S(1)} %compare_and_fusion.2, bf16[256,1,8,128]{3,0,2,1:T(8,128)(2,1)S(1)} %get-tuple-element.370, bf16[8192,1,128]{2,0,1:T(8,128)(2,1)} %get-tuple-element.369, s32[]{:T(128)S(6)} %select_n.59), kind=kOutput, calls=%fused_computation.3.clone.1 | convolution fusion | flops 543160320 | bytes 9445380 | tf_op jit(solution)/shard_map/while/body/eval_jaxpr/qhgd,khd->hgqk/dot_general | solution.py:33
  189.8 5.0 %fusion.35 = f32[1,8,256,128]{3,2,1,0:T(8,128)S(1)} fusion(f32[1,8,256,128]{3,2,1,0:T(8,128)S(1)} %get-tuple-element.349, f32[8,256]{1,0:T(8,128)S(1)} %get-tuple-element.330, pred[]{:T(512)S(6)} %compare.3, bf16[8192,1,128]{2,0,1:T(8,128)(2,1)} %get-tuple-element.371, s32[]{:T(128)S(6)} %select_n.59, f32[1024,256,8]{1,0,2:T(8,128)} %get-tuple-element.329, ...), kind=kOutput, calls=%fused_computation.7.clone.1 | convolution fusion | flops 548143104 | bytes 11026437 | tf_op jit(solution)/shard_map/while/body/eval_jaxpr/hgqk,khd->hgqd/dot_general | solution.py:43
  198.9 5.6 %fusion.33 = (f32[8,256]{1,0:T(8,128)S(1)}, f32[1024,256,8]{1,0,2:T(8,128)}) fusion(pred[256,1024]{0,1:T(8,128)(4,1)S(1)} %compare_and_fusion.2, bf16[256,1,8,128]{3,0,2,1:T(8,128)(2,1)S(1)} %get-tuple-element.370, bf16[8192,1,128]{2,0,1:T(8,128)(2,1)} %get-tuple-element.369, s32[]{:T(128)S(6)} %select_n.59), kind=kOutput, calls=%fused_computation.3.clone.1 | convolution fusion | flops 543160320 | bytes 9445380 | tf_op jit(solution)/shard_map/while/body/eval_jaxpr/qhgd,khd->hgqk/dot_general | solution.py:33
  204.5 5.0 %fusion.35 = f32[1,8,256,128]{3,2,1,0:T(8,128)S(1)} fusion(f32[1,8,256,128]{3,2,1,0:T(8,128)S(1)} %get-tuple-element.349, f32[8,256]{1,0:T(8,128)S(1)} %get-tuple-element.330, pred[]{:T(512)S(6)} %compare.3, bf16[8192,1,128]{2,0,1:T(8,128)(2,1)} %get-tuple-element.371, s32[]{:T(128)S(6)} %select_n.59, f32[1024,256,8]{1,0,2:T(8,128)} %get-tuple-element.329, ...), kind=kOutput, calls=%fused_computation.7.clone.1 | convolution fusion | flops 548143104 | bytes 11026437 | tf_op jit(solution)/shard_map/while/body/eval_jaxpr/hgqk,khd->hgqd/dot_general | solution.py:43
  213.5 5.6 %fusion.33 = (f32[8,256]{1,0:T(8,128)S(1)}, f32[1024,256,8]{1,0,2:T(8,128)}) fusion(pred[256,1024]{0,1:T(8,128)(4,1)S(1)} %compare_and_fusion.2, bf16[256,1,8,128]{3,0,2,1:T(8,128)(2,1)S(1)} %get-tuple-element.370, bf16[8192,1,128]{2,0,1:T(8,128)(2,1)} %get-tuple-element.369, s32[]{:T(128)S(6)} %select_n.59), kind=kOutput, calls=%fused_computation.3.clone.1 | convolution fusion | flops 543160320 | bytes 9445380 | tf_op jit(solution)/shard_map/while/body/eval_jaxpr/qhgd,khd->hgqk/dot_general | solution.py:33
  219.1 5.0 %fusion.35 = f32[1,8,256,128]{3,2,1,0:T(8,128)S(1)} fusion(f32[1,8,256,128]{3,2,1,0:T(8,128)S(1)} %get-tuple-element.349, f32[8,256]{1,0:T(8,128)S(1)} %get-tuple-element.330, pred[]{:T(512)S(6)} %compare.3, bf16[8192,1,128]{2,0,1:T(8,128)(2,1)} %get-tuple-element.371, s32[]{:T(128)S(6)} %select_n.59, f32[1024,256,8]{1,0,2:T(8,128)} %get-tuple-element.329, ...), kind=kOutput, calls=%fused_computation.7.clone.1 | convolution fusion | flops 548143104 | bytes 11026437 | tf_op jit(solution)/shard_map/while/body/eval_jaxpr/hgqk,khd->hgqd/dot_general | solution.py:43
  228.2 5.6 %fusion.33 = (f32[8,256]{1,0:T(8,128)S(1)}, f32[1024,256,8]{1,0,2:T(8,128)}) fusion(pred[256,1024]{0,1:T(8,128)(4,1)S(1)} %compare_and_fusion.2, bf16[256,1,8,128]{3,0,2,1:T(8,128)(2,1)S(1)} %get-tuple-element.370, bf16[8192,1,128]{2,0,1:T(8,128)(2,1)} %get-tuple-element.369, s32[]{:T(128)S(6)} %select_n.59), kind=kOutput, calls=%fused_computation.3.clone.1 | convolution fusion | flops 543160320 | bytes 9445380 | tf_op jit(solution)/shard_map/while/body/eval_jaxpr/qhgd,khd->hgqk/dot_general | solution.py:33
  233.8 5.0 %fusion.35 = f32[1,8,256,128]{3,2,1,0:T(8,128)S(1)} fusion(f32[1,8,256,128]{3,2,1,0:T(8,128)S(1)} %get-tuple-element.349, f32[8,256]{1,0:T(8,128)S(1)} %get-tuple-element.330, pred[]{:T(512)S(6)} %compare.3, bf16[8192,1,128]{2,0,1:T(8,128)(2,1)} %get-tuple-element.371, s32[]{:T(128)S(6)} %select_n.59, f32[1024,256,8]{1,0,2:T(8,128)} %get-tuple-element.329, ...), kind=kOutput, calls=%fused_computation.7.clone.1 | convolution fusion | flops 548143104 | bytes 11026437 | tf_op jit(solution)/shard_map/while/body/eval_jaxpr/hgqk,khd->hgqd/dot_general | solution.py:43
  242.8 5.6 %fusion.33 = (f32[8,256]{1,0:T(8,128)S(1)}, f32[1024,256,8]{1,0,2:T(8,128)}) fusion(pred[256,1024]{0,1:T(8,128)(4,1)S(1)} %compare_and_fusion.2, bf16[256,1,8,128]{3,0,2,1:T(8,128)(2,1)S(1)} %get-tuple-element.370, bf16[8192,1,128]{2,0,1:T(8,128)(2,1)} %get-tuple-element.369, s32[]{:T(128)S(6)} %select_n.59), kind=kOutput, calls=%fused_computation.3.clone.1 | convolution fusion | flops 543160320 | bytes 9445380 | tf_op jit(solution)/shard_map/while/body/eval_jaxpr/qhgd,khd->hgqk/dot_general | solution.py:33
  248.4 5.0 %fusion.35 = f32[1,8,256,128]{3,2,1,0:T(8,128)S(1)} fusion(f32[1,8,256,128]{3,2,1,0:T(8,128)S(1)} %get-tuple-element.349, f32[8,256]{1,0:T(8,128)S(1)} %get-tuple-element.330, pred[]{:T(512)S(6)} %compare.3, bf16[8192,1,128]{2,0,1:T(8,128)(2,1)} %get-tuple-element.371, s32[]{:T(128)S(6)} %select_n.59, f32[1024,256,8]{1,0,2:T(8,128)} %get-tuple-element.329, ...), kind=kOutput, calls=%fused_computation.7.clone.1 | convolution fusion | flops 548143104 | bytes 11026437 | tf_op jit(solution)/shard_map/while/body/eval_jaxpr/hgqk,khd->hgqd/dot_general | solution.py:43
  257.5 5.6 %fusion.33 = (f32[8,256]{1,0:T(8,128)S(1)}, f32[1024,256,8]{1,0,2:T(8,128)}) fusion(pred[256,1024]{0,1:T(8,128)(4,1)S(1)} %compare_and_fusion.2, bf16[256,1,8,128]{3,0,2,1:T(8,128)(2,1)S(1)} %get-tuple-element.370, bf16[8192,1,128]{2,0,1:T(8,128)(2,1)} %get-tuple-element.369, s32[]{:T(128)S(6)} %select_n.59), kind=kOutput, calls=%fused_computation.3.clone.1 | convolution fusion | flops 543160320 | bytes 9445380 | tf_op jit(solution)/shard_map/while/body/eval_jaxpr/qhgd,khd->hgqk/dot_general | solution.py:33
  263.1 5.0 %fusion.35 = f32[1,8,256,128]{3,2,1,0:T(8,128)S(1)} fusion(f32[1,8,256,128]{3,2,1,0:T(8,128)S(1)} %get-tuple-element.349, f32[8,256]{1,0:T(8,128)S(1)} %get-tuple-element.330, pred[]{:T(512)S(6)} %compare.3, bf16[8192,1,128]{2,0,1:T(8,128)(2,1)} %get-tuple-element.371, s32[]{:T(128)S(6)} %select_n.59, f32[1024,256,8]{1,0,2:T(8,128)} %get-tuple-element.329, ...), kind=kOutput, calls=%fused_computation.7.clone.1 | convolution fusion | flops 548143104 | bytes 11026437 | tf_op jit(solution)/shard_map/while/body/eval_jaxpr/hgqk,khd->hgqd/dot_general | solution.py:43
  271.9 16.8 %all_to_all.71 = bf16[256,8,128]{2,1,0:T(8,128)(2,1)S(1)} all-to-all(bf16[256,8,128]{2,1,0:T(8,128)(2,1)S(1)} %fusion.19), channel_id=1, replica_groups=mesh['kv'=8,'ctx'=32] {'kv'}, dimensions={0} | all-to-all | bytes 1048576 | tf_op jit(solution)/shard_map/all_to_all | solution.py:102
  (95 shorter events, 41.6 us)
Async XLA Ops:
  6.5 81.2 %all-gather.3.cloned.1.call-start = ((), (), s32[]{:S(2)}) async-start(), calls=%async_computation.4 | async-start | bytes 2162688 | tf_op jit(solution)/shard_map/all_gather | solution.py:81
  22.3 131.6 %all-gather.5.cloned.1.call-start = ((), (), s32[]{:S(2)}) async-start(), calls=%async_computation.5 | async-start | bytes 2162688 | tf_op jit(solution)/shard_map/all_gather | solution.py:82
  36.0 13.5 %all-to-all-start.1 = ((bf16[32,64,128]{2,0,1:T(8,128)(2,1)}), bf16[32,64,128]{2,0,1:T(8,128)(2,1)S(1)}, u32[]{:S(2)}, u32[]{:S(2)}) async-start(bf16[32,64,128]{2,0,1:T(8,128)(2,1)} %multiply_convert_fusion), calls=%async_computation.1 | async-start | bytes 1048576 | tf_op jit(solution)/shard_map/all_to_all | solution.py:66
  160.6 5.9 %copy-start = (f32[1024,256,8]{1,0,2:T(8,128)S(1)}, f32[1024,256,8]{1,0,2:T(8,128)}, u32[]{:S(2)}) copy-start(f32[1024,256,8]{1,0,2:T(8,128)} %get-tuple-element.329) | copy-start | bytes 25165828 | tf_op jit(solution)/shard_map/while
  175.2 5.9 %copy-start = (f32[1024,256,8]{1,0,2:T(8,128)S(1)}, f32[1024,256,8]{1,0,2:T(8,128)}, u32[]{:S(2)}) copy-start(f32[1024,256,8]{1,0,2:T(8,128)} %get-tuple-element.329) | copy-start | bytes 25165828 | tf_op jit(solution)/shard_map/while
  189.8 5.9 %copy-start = (f32[1024,256,8]{1,0,2:T(8,128)S(1)}, f32[1024,256,8]{1,0,2:T(8,128)}, u32[]{:S(2)}) copy-start(f32[1024,256,8]{1,0,2:T(8,128)} %get-tuple-element.329) | copy-start | bytes 25165828 | tf_op jit(solution)/shard_map/while
  204.5 5.9 %copy-start = (f32[1024,256,8]{1,0,2:T(8,128)S(1)}, f32[1024,256,8]{1,0,2:T(8,128)}, u32[]{:S(2)}) copy-start(f32[1024,256,8]{1,0,2:T(8,128)} %get-tuple-element.329) | copy-start | bytes 25165828 | tf_op jit(solution)/shard_map/while
  219.1 5.9 %copy-start = (f32[1024,256,8]{1,0,2:T(8,128)S(1)}, f32[1024,256,8]{1,0,2:T(8,128)}, u32[]{:S(2)}) copy-start(f32[1024,256,8]{1,0,2:T(8,128)} %get-tuple-element.329) | copy-start | bytes 25165828 | tf_op jit(solution)/shard_map/while
  233.8 5.9 %copy-start = (f32[1024,256,8]{1,0,2:T(8,128)S(1)}, f32[1024,256,8]{1,0,2:T(8,128)}, u32[]{:S(2)}) copy-start(f32[1024,256,8]{1,0,2:T(8,128)} %get-tuple-element.329) | copy-start | bytes 25165828 | tf_op jit(solution)/shard_map/while
  248.4 5.9 %copy-start = (f32[1024,256,8]{1,0,2:T(8,128)S(1)}, f32[1024,256,8]{1,0,2:T(8,128)}, u32[]{:S(2)}) copy-start(f32[1024,256,8]{1,0,2:T(8,128)} %get-tuple-element.329) | copy-start | bytes 25165828 | tf_op jit(solution)/shard_map/while
  263.1 5.9 %copy-start = (f32[1024,256,8]{1,0,2:T(8,128)S(1)}, f32[1024,256,8]{1,0,2:T(8,128)}, u32[]{:S(2)}) copy-start(f32[1024,256,8]{1,0,2:T(8,128)} %get-tuple-element.329) | copy-start | bytes 25165828 | tf_op jit(solution)/shard_map/while
Sparse Core Ops, SparseCore 0:
  22.4 65.2 all-gather.2
  89.5 64.3 all-gather.4
where the time goes:
time: 297 us; the launch traced here: 296 us
  waiting for transfers between devices  112 us (38%)
  matrix products  85 us (29%)
  blocking collectives  40.6 us (14%)
  other arithmetic  25.4 us (9%)
  local copies, waits for them, and re-layouts  16.1 us (5%)
  between operations  13.5 us (5%)
  starting transfers between devices  3.54 us (1%)
    all_gather x1, waiting for transfers between devices, shards(): piece_values = lax.all_gather(my_values, 'ctx', axis=0, tiled=True)  66.2 us
    dot_general x8, matrix products, merge_block(): jnp.einsum('qhgd,khd->hgqk', grouped, key_block, preferred_element_type=j...  44.8 us
    dot_general x8, matrix products, merge_block(): jnp.einsum('hgqk,khd->hgqd', weights, value_block, preferred_element_type...  40.2 us
    all_gather x1, waiting for transfers between devices, shards(): piece_keys = lax.all_gather(my_keys, 'ctx', axis=0, tiled=True)  38.2 us
    all_to_all x1, blocking collectives, shards(): return lax.all_to_all(result, 'kv', split_axis=0, concat_axis=1, tiled=True)  16.8 us
    reduce_sum x8, other arithmetic, merge_block(): jnp.sum(weights.astype(jnp.float32), axis=-1)  16 us
    all_to_all x1, blocking collectives, shards(): lax.all_to_all(coded, 'kv', split_axis=1, concat_axis=0, tiled=True)  14.1 us
    all_to_all x1, blocking collectives, shards(): lax.all_to_all(values, 'kv', split_axis=1, concat_axis=0, tiled=True)  9.76 us
  transfers between devices with their start and end apart: 3, of which 3 were waited for; matrix products, arithmetic and copies ran while one was open for 2% of the time, Pallas kernels for 0%

commit v1 on v0

v1 whole, which is shorter than its diff:
```python
import jax
import jax.numpy as jnp
from jax import lax
from jax.experimental import pallas as pl
from jax.experimental.pallas import tpu as pltpu
from jax.sharding import PartitionSpec as P

MESH = pl.DeviceIdType.MESH
TOK = 32
HEADS = 8
GROUP = 8
DIM = 128
BLOCKS = 256
REACH = 64
WIN = (REACH + 1) * TOK
PAD = 2176
CHUNK = 256
FACTOR = DIM**-0.5 * 1.4426950408889634
LOW = -1e30


def spot(x, y, z, core):
    return (y * 2 + x // 2, z * 4 + (x % 2) * 2 + core)


def kernel(
    order, block_pos, doc_lengths, q_ref, k_ref, v_ref, off_ref, smooth_ref, scale_ref, out_ref,
    rows, kv_send, kv_all, q_send, q_all, o_send, o_all, thr, kwin, vwin, scores,
    kvs, kvr, qs, qr, os, orr, gs, gr,
):
    kv = lax.axis_index("kv")
    ctx = lax.axis_index("ctx")
    y, z, core = kv // 2, ctx // 4, ctx % 2
    x = (kv % 2) * 2 + (ctx // 2) % 2

    def along_z(o):
        return spot(x, y, lax.rem(z + o, 8), core)

    x_next = [spot((x + d) % 4, y, z, core) for d in (1, 3)]
    y_next = [spot(x, (y + d) % 4, z, core) for d in (1, 3)]
    twin = spot(x, y, z, 1 - core)
    greeted = [along_z(o) for o in range(1, 8)] + x_next + y_next + [twin]
    barrier = pltpu.get_barrier_semaphore()
    for peer in greeted:
        pl.semaphore_signal(barrier, inc=1, device_id=peer, device_id_type=MESH)

    exps = smooth_ref[...] + scale_ref[...]
    up = jnp.left_shift(jnp.int32(1), -exps).astype(jnp.float32)
    down = jnp.left_shift(jnp.int32(1), exps + 7).astype(jnp.float32) * (2.0**-7)
    codes = jnp.floor(
        k_ref[...].astype(jnp.float32) * up[None] + off_ref[...].astype(jnp.float32) * (1.0 / 256)
    )
    coded = jnp.clip(codes, -128.0, 127.0) * down[None]
    rows[0] = coded.reshape(TOK * HEADS, DIM)
    rows[1] = v_ref[...].astype(jnp.float32).reshape(TOK * HEADS, DIM)
    for h in range(HEADS):
        for t in range(2):
            kv_send[h, t] = rows[t, pl.ds(h, TOK, stride=HEADS), :].astype(jnp.bfloat16)

    pl.semaphore_wait(barrier, len(greeted))

    far_first = (4, 3, 5, 2, 6, 1, 7)
    kv_copies = []
    for o in far_first:
        c = pltpu.make_async_remote_copy(
            kv_send.at[lax.rem(z + o, 8)], kv_all.at[core, y, x, 8 - o],
            kvs.at[o], kvr.at[8 - o], device_id=along_z(o), device_id_type=MESH,
        )
        c.start()
        kv_copies.append(c)
    kv_all[core, y, x, 0] = kv_send[z]

    for g in range(HEADS // 2):
        pair = q_ref[:, 16 * g : 16 * g + 16, :].astype(jnp.float32)
        for i in range(2):
            q_send[2 * g + i] = (
                pair[:, 8 * i : 8 * i + 8, :].reshape(TOK * GROUP, DIM).astype(jnp.bfloat16)
            )
    q_copies = []
    for o in far_first:
        c = pltpu.make_async_remote_copy(
            q_send.at[lax.rem(z + o, 8)], q_all.at[8 - o],
            qs.at[o], qr.at[8 - o], device_id=along_z(o), device_id_type=MESH,
        )
        c.start()
        q_copies.append(c)
    q_all[0] = q_send[z]

    def block_at(o):
        return block_pos[lax.rem(z + o, 8) * 32 + (x % 2) * 16 + core * 8 + y * 2 + x // 2]

    def starts(o, carry):
        base = block_at(o) * TOK
        pos = base + lax.broadcasted_iota(jnp.int32, (TOK * GROUP, DIM), 0) // GROUP
        first = jnp.zeros((TOK * GROUP, DIM), jnp.int32)
        end = jnp.int32(0)
        for d in range(15):
            end = end + doc_lengths[d]
            first = jnp.where(pos >= end, end, first)
        thr[o] = first - (base - REACH * TOK)
        return carry

    lax.fori_loop(0, 8, starts, 0)
    vwin[:, DIM:] = jnp.ones((PAD, DIM), jnp.bfloat16)
    vwin[WIN:, :DIM] = jnp.zeros((PAD - WIN, DIM), jnp.bfloat16)
    kwin[WIN:] = jnp.zeros((PAD - WIN, DIM), jnp.bfloat16)

    for c in kv_copies:
        c.wait_recv()

    sends = []

    def send(ref, target):
        i = len(sends)
        c = pltpu.make_async_remote_copy(
            ref, ref, gs.at[i], gr.at[i], device_id=target, device_id_type=MESH
        )
        c.start()
        sends.append(c)
        return c

    nexts = {"x": x_next, "y": y_next}
    parts = (("x", "y", 0), ("y", "x", 4))

    def piece(rel, lo, n):
        return kv_all.at[core, (y + rel[1] + 4) % 4, (x + rel[0] + 4) % 4, pl.ds(lo, n)]

    def both(axis, rel, lo):
        return [send(piece(rel, lo, 4), target) for target in nexts[axis]]

    def moved(rel, axis, d):
        return (rel[0] + d, rel[1]) if axis == "x" else (rel[0], rel[1] + d)

    def pass_on(axis, rel, lo, copies):
        copies[0].wait_recv()
        a = send(piece(moved(rel, axis, -1), lo, 2), nexts[axis][0])
        copies[1].wait_recv()
        b = send(piece(moved(rel, axis, 1), lo + 2, 2), nexts[axis][1])
        return [a, b]

    twin_copies = []

    def line_to_twin(second, rel, lo):
        if second == "y":
            ref = kv_all.at[core, :, (x + rel[0] + 4) % 4, pl.ds(lo, 4)]
        else:
            ref = kv_all.at[core, (y + rel[1] + 4) % 4, :, pl.ds(lo, 4)]
        twin_copies.append(send(ref, twin))

    one = [both(p[0], (0, 0), p[2]) for p in parts]
    two = [(p, (0, 0), both(p[1], (0, 0), p[2])) for p in parts]
    opposite = [pass_on(p[0], (0, 0), p[2], c) for p, c in zip(parts, one)]
    for d in (-1, 1):
        for p in parts:
            rel = moved((0, 0), p[0], d)
            two.append((p, rel, both(p[1], rel, p[2])))
    last = []

    def second(entry):
        p, rel, copies = entry
        last.append((p, rel, pass_on(p[1], rel, p[2], copies)))

    def finish(entry):
        p, rel, copies = entry
        for c in copies:
            c.wait_recv()
        line_to_twin(p[1], rel, p[2])

    second(two[0])
    second(two[1])
    for p, copies in zip(parts, opposite):
        for c in copies:
            c.wait_recv()
        rel = moved((0, 0), p[0], 2)
        two.append((p, rel, both(p[1], rel, p[2])))
    for i in range(2, len(two)):
        second(two[i])
        finish(last[i - 2])
    for entry in last[len(two) - 2 :]:
        finish(entry)
    for c in twin_copies:
        c.wait_recv()
    for c in q_copies:
        c.wait_recv()

    lane = lax.broadcasted_iota(jnp.int32, (TOK * GROUP, DIM), 1)
    row = lax.broadcasted_iota(jnp.int32, (TOK * GROUP, DIM), 0)
    causal = lane <= row // GROUP

    def attend(j, carry):
        half, odd = j // 2, j % 2
        o = 4 + half - odd * (1 + 2 * half)
        pos = block_at(o)

        def fetch(i, c):
            for u in range(5):
                b = order[pos + i * 5 + u]
                src = kv_all.at[b // 128, (b // 32) % 4, (b // 8) % 4, b % 8]
                at = pl.ds(pl.multiple_of((i * 5 + u) * TOK, TOK), TOK)
                kwin[at, :] = src[0]
                vwin[at, pl.ds(0, DIM)] = src[1]
            return c

        lax.fori_loop(0, (REACH + 1) // 5, fetch, 0)
        q = q_all[o]
        first = thr[o]
        top = jnp.full((TOK * GROUP, DIM), LOW, jnp.float32)
        for c0 in range(0, PAD, CHUNK):
            width = min(CHUNK, PAD - c0)
            s = lax.dot_general(
                q, kwin[c0 : c0 + width, :], (((1,), (1,)), ((), ())),
                preferred_element_type=jnp.float32,
            )
            for t in range(0, width, DIM):
                ok = lane + (c0 + t) >= first
                if c0 + t == REACH * TOK:
                    ok = ok & causal
                tile = jnp.where(ok, s[:, t : t + DIM], LOW)
                scores[:, c0 + t : c0 + t + DIM] = tile
                top = jnp.maximum(top, tile)
        peak = jnp.max(top, axis=1, keepdims=True)
        total = jnp.zeros((TOK * GROUP, 2 * DIM), jnp.float32)
        for c0 in range(0, PAD, CHUNK):
            width = min(CHUNK, PAD - c0)
            w = jnp.exp2((scores[:, c0 : c0 + width] - peak) * FACTOR).astype(jnp.bfloat16)
            total = total + jnp.dot(
                w, vwin[c0 : c0 + width, :], preferred_element_type=jnp.float32
            )
        result = (total[:, :DIM] / total[:, DIM:]).astype(jnp.bfloat16)
        o_send[o] = result

        @pl.when(j < 7)
        def _():
            pltpu.make_async_remote_copy(
                o_send.at[o], o_all.at[z], os.at[o], orr.at[lax.rem(8 - o, 8)],
                device_id=along_z(o), device_id_type=MESH,
            ).start()

        return carry

    lax.fori_loop(0, 8, attend, 0)
    o_all[z] = o_send[0]
    for o in far_first:
        pltpu.make_async_remote_copy(
            o_send.at[o], o_all.at[z], os.at[o], orr.at[8 - o],
            device_id=along_z(o), device_id_type=MESH,
        ).wait_recv()
    for g in range(HEADS // 2):
        pair = [
            o_all[2 * g + i].astype(jnp.float32).reshape(TOK, GROUP, DIM) for i in range(2)
        ]
        out_ref[:, 16 * g : 16 * g + 16, :] = jnp.concatenate(pair, axis=1).astype(jnp.bfloat16)
    for c in kv_copies + q_copies + sends:
        c.wait_send()
    for o in far_first:
        pltpu.make_async_remote_copy(
            o_send.at[o], o_all.at[z], os.at[o], orr.at[8 - o],
            device_id=along_z(o), device_id_type=MESH,
        ).wait_send()


def shards(queries, keys, values, offsets, smooth_exp, scale_exp, placement, doc_lengths):
    z = lax.axis_index("ctx") // 4
    block_pos = placement.reshape(BLOCKS, TOK)[:, 0] // TOK
    b = jnp.arange(BLOCKS, dtype=jnp.int32)
    ctx, kv = b // 8, b % 8
    x = (kv % 2) * 2 + (ctx // 2) % 2
    place = (((ctx % 2) * 4 + kv // 2) * 4 + x) * 8 + (ctx // 4 - z) % 8
    order = jnp.sum(
        jnp.where(block_pos[None, :] == b[:, None], place[None, :], 0), axis=1
    ).astype(jnp.int32)
    order = jnp.concatenate([jnp.zeros((REACH,), jnp.int32), order])
    bf, f32 = jnp.bfloat16, jnp.float32
    dma = pltpu.SemaphoreType.DMA
    smem = pl.BlockSpec(memory_space=pltpu.SMEM)
    vmem = pl.BlockSpec(memory_space=pltpu.VMEM)
    n_rows = TOK * GROUP
    return pl.pallas_call(
        kernel,
        out_shape=jax.ShapeDtypeStruct(queries.shape, bf),
        in_specs=[smem] * 3 + [vmem] * 6,
        out_specs=vmem,
        scratch_shapes=[
            pltpu.VMEM((2, TOK * HEADS, DIM), f32),
            pltpu.VMEM((HEADS, 2, TOK, DIM), bf),
            pltpu.VMEM((2, 4, 4, 8, 2, TOK, DIM), bf),
            pltpu.VMEM((HEADS, n_rows, DIM), bf),
            pltpu.VMEM((8, n_rows, DIM), bf),
            pltpu.VMEM((8, n_rows, DIM), bf),
            pltpu.VMEM((HEADS, n_rows, DIM), bf),
            pltpu.VMEM((8, n_rows, DIM), jnp.int32),
            pltpu.VMEM((PAD, DIM), bf),
            pltpu.VMEM((PAD, 2 * DIM), bf),
            pltpu.VMEM((n_rows, PAD), f32),
            dma((8,)), dma((8,)), dma((8,)), dma((8,)), dma((8,)), dma((8,)),
            dma((48,)), dma((48,)),
        ],
        compiler_params=pltpu.CompilerParams(
            collective_id=0, has_side_effects=True, vmem_limit_bytes=40 * 2**20
        ),
        name="attend",
    )(order, block_pos, doc_lengths, queries, keys, values, offsets, smooth_exp, scale_exp)


def solution(mesh):
    tokens = P(("ctx", "kv"), None, None)
    return jax.shard_map(
        shards,
        mesh=mesh,
        in_specs=(tokens,) * 4 + (P(),) * 4,
        out_specs=tokens,
        check_vma=False,
    )
```

time: 297 us -> 69 us (0.23)
  waiting for transfers between devices: 112 us -> 0 us
  matrix products: 85 us -> 0 us
  Pallas kernels: 0 us -> 65.2 us
  blocking collectives: 40.6 us -> 0 us
  other arithmetic: 25.4 us -> 0.14 us
  between operations: 13.5 us -> 0.08 us
  local copies, waits for them, and re-layouts: 16.1 us -> 3.38 us
  starting transfers between devices: 3.54 us -> 0 us
    all_gather x2 -> x0, waiting for transfers between devices: 104 us -> none  [the longest x1 66.2 us: shards(): piece_values = lax.all_gather(my_values, 'ctx', axis=0, tiled=True)]
    dot_general x16 -> x0, matrix products: 85 us -> none  [the longest x8 44.8 us: merge_block(): jnp.einsum('qhgd,khd->hgqk', grouped, key_block, preferred_element_type=j...]
    pallas_call x0 -> x1, Pallas kernels: none -> 65.2 us  [shards(): pl.pallas_call(kernel, out_shape=jax.ShapeDtypeStruct(queries.shape, bf),...]
    all_to_all x3 -> x0, blocking collectives: 40.6 us -> none  [the longest x1 16.8 us: shards(): return lax.all_to_all(result, 'kv', split_axis=0, concat_axis=1, tiled=True)]
    reduce_sum x10 -> x1, other arithmetic: 17 us -> 0.12 us  [shards(): jnp.sum(jnp.where(block_pos[None, :] == b[:, None], place[None, :], 0), a...]
    all_to_all x1 -> x0, waiting for transfers between devices: 7.25 us -> none  [shards(): lax.all_to_all(scaled, 'kv', split_axis=1, concat_axis=0, tiled=True)]
    while x24 -> x0, local copies, waits for them, and re-layouts: 7.06 us -> none
    dynamic_slice x17 -> x0, local copies, waits for them, and re-layouts: 6.37 us -> none  [the longest x8 5.55 us: advance(): pos_key = lax.dynamic_slice_in_dim(placement, offset, block_rows, 0)]
  transfers between devices with their start and end apart: 3 -> 0, of which waited for: 3 -> 0; matrix products, arithmetic and copies ran while one was open for 2% -> 0% of each run, Pallas kernels for 0% -> 0%
where the time goes in v1:
time: 69 us; the launch traced here: 68.8 us
  Pallas kernels  65.2 us (94%)
  local copies, waits for them, and re-layouts  3.38 us (5%)
    pallas_call x1, Pallas kernels, shards(): pl.pallas_call(kernel, out_shape=jax.ShapeDtypeStruct(queries.shape, bf),...  65.2 us
    unnamed x17, local copies, waits for them, and re-layouts  3.12 us

profile of v1, /device:TPU:1, one launch (start us, length us, event | category | flops | bytes accessed | tf_op | source)
XLA Modules:
  0.0 68.8 jit_solution(15137437751639531040)
XLA Ops:
  0.0 0.0 copy-start.7
  0.0 0.8 %copy-done.7 = s32[8192]{0:T(1024)S(1)} copy-done((s32[8192]{0:T(1024)S(1)}, s32[8192]{0:T(1024)}, u32[]{:S(2)}) %copy-start.7) | copy-done | bytes 32792
  0.8 0.0 copy-start.1
  0.8 0.1 reshape.144
  0.8 0.0 copy-start.2
  0.9 0.0 copy-start.3
  0.9 0.1 slice_reduce_fusion
  1.0 0.0 copy-start.6
  1.0 0.0 copy-start.4
  1.0 0.0 copy-start.5
  1.0 0.1 select_reduce_fusion
  1.2 0.1 concatenate.3.order
  1.2 0.4 copy-done.1
  1.7 0.0 copy-done.2
  1.7 0.0 copy-done.3
  1.7 0.0 copy-done.6
  1.7 0.0 copy-done.4
  1.7 0.0 copy-done.5
  1.7 0.0 copy-start
  1.8 1.0 %copy-done = bf16[32,64,128]{2,1,0:T(8,128)(2,1)S(1)} copy-done((bf16[32,64,128]{2,1,0:T(8,128)(2,1)S(1)}, bf16[32,64,128]{2,1,0:T(8,128)(2,1)}, u32[]{:S(2)}) %copy-start) | copy-done | bytes 524312
  2.8 65.2 %attend.1 = bf16[32,64,128]{2,1,0:T(8,128)(2,1)S(1)} custom-call(s32[320]{0:T(512)S(1)} %concatenate.3.order, s32[256]{0:T(256)S(1)} %get-tuple-element.5.block_pos, s32[16]{0:T(128)S(1)} %copy-done.6, bf16[32,64,128]{2,1,0:T(8,128)(2,1)S(1)} %copy-done, bf16[32,8,128]{2,1,0:T(8,128)(2,1)S(1)} %copy-done.2, bf16[32,8,128]{2,1,0:T(8,128)(2,1)S(1)} %copy-done.3, ...), custom_call_target="tpu_custom_call" | custom-call | tf_op jit(solution)/shard_map/attend/pallas_call | solution.py:278
  68.0 0.8 %copy.10 = bf16[32,64,128]{2,1,0:T(8,128)(2,1)} copy(bf16[32,64,128]{2,1,0:T(8,128)(2,1)S(1)} %attend.1) | data formatting | bytes 1048576
  (1 shorter events, 0.0 us)
Async XLA Ops:
  0.0 0.8 %copy-start.7 = (s32[8192]{0:T(1024)S(1)}, s32[8192]{0:T(1024)}, u32[]{:S(2)}) copy-start(s32[8192]{0:T(1024)} %param.14) | copy-start | bytes 98308
  0.8 0.9 %copy-start.1 = (s32[32,8,128]{2,1,0:T(8,128)S(1)}, s32[32,8,128]{2,1,0:T(8,128)}, u32[]{:S(2)}) copy-start(s32[32,8,128]{2,1,0:T(8,128)} %off_ref.1) | copy-start | bytes 393220
  0.8 0.9 %copy-start.2 = (bf16[32,8,128]{2,1,0:T(8,128)(2,1)S(1)}, bf16[32,8,128]{2,1,0:T(8,128)(2,1)}, u32[]{:S(2)}) copy-start(bf16[32,8,128]{2,1,0:T(8,128)(2,1)} %k_ref.1) | copy-start | bytes 196612
  0.9 0.9 %copy-start.3 = (bf16[32,8,128]{2,1,0:T(8,128)(2,1)S(1)}, bf16[32,8,128]{2,1,0:T(8,128)(2,1)}, u32[]{:S(2)}) copy-start(bf16[32,8,128]{2,1,0:T(8,128)(2,1)} %v_ref.1) | copy-start | bytes 196612
  1.0 0.8 %copy-start.6 = (s32[16]{0:T(128)S(1)}, s32[16]{0:T(128)}, u32[]{:S(2)}) copy-start(s32[16]{0:T(128)} %doc_lengths.1) | copy-start | bytes 196
  1.0 0.7 %copy-start.4 = (s32[8,128]{1,0:T(8,128)S(1)}, s32[8,128]{1,0:T(8,128)}, u32[]{:S(2)}) copy-start(s32[8,128]{1,0:T(8,128)} %smooth_ref.1) | copy-start | bytes 12292
  1.0 0.7 %copy-start.5 = (s32[8,128]{1,0:T(8,128)S(1)}, s32[8,128]{1,0:T(8,128)}, u32[]{:S(2)}) copy-start(s32[8,128]{1,0:T(8,128)} %scale_ref.1) | copy-start | bytes 12292
  1.7 1.0 %copy-start = (bf16[32,64,128]{2,1,0:T(8,128)(2,1)S(1)}, bf16[32,64,128]{2,1,0:T(8,128)(2,1)}, u32[]{:S(2)}) copy-start(bf16[32,64,128]{2,1,0:T(8,128)(2,1)} %q_ref.1) | copy-start | bytes 1572868

commit v2 on v1

--- a/solution.py
+++ b/solution.py
@@ -12,9 +12,12 @@
 DIM = 128
 BLOCKS = 256
 REACH = 64
-WIN = (REACH + 1) * TOK
 PAD = 2176
 CHUNK = 256
+N_ROWS = TOK * GROUP
+SORTED = REACH + BLOCKS + 8
+DOCS = 16
+BIG = 65536.0
 FACTOR = DIM**-0.5 * 1.4426950408889634
 LOW = -1e30
 
@@ -24,10 +27,21 @@
 
 
 def kernel(
-    order, block_pos, doc_lengths, q_ref, k_ref, v_ref, off_ref, smooth_ref, scale_ref, out_ref,
-    rows, kv_send, kv_all, q_send, q_all, o_send, o_all, thr, kwin, vwin, scores,
-    kvs, kvr, qs, qr, os, orr, gs, gr,
+    place_hbm, docs_hbm, q_hbm, k_hbm, v_hbm, off_hbm, smooth_hbm, scale_hbm, out_ref,
+    place_v, place_s, docs_s, q_ref, k_ref, v_ref, off_ref, smooth_ref, scale_ref, order_v, order,
+    rows, kv_send, kv_all, q_send, q_all, q_doc, o_send, o_all, keys, vals, scores,
+    kvs, kvr, qs, qr, os, orr, gs, gr, ins,
 ):
+    loads = []
+    pairs = (
+        (k_hbm, k_ref), (off_hbm, off_ref), (smooth_hbm, smooth_ref), (scale_hbm, scale_ref),
+        (v_hbm, v_ref), (q_hbm, q_ref), (docs_hbm, docs_s), (place_hbm, place_v),
+        (place_hbm, place_s),
+    )
+    for i, (src, dst) in enumerate(pairs):
+        c = pltpu.make_async_copy(src, dst, ins.at[i])
+        c.start()
+        loads.append(c)
     kv = lax.axis_index("kv")
     ctx = lax.axis_index("ctx")
     y, z, core = kv // 2, ctx // 4, ctx % 2
@@ -44,6 +58,8 @@
     for peer in greeted:
         pl.semaphore_signal(barrier, inc=1, device_id=peer, device_id_type=MESH)
 
+    for c in loads[:5]:
+        c.wait()
     exps = smooth_ref[...] + scale_ref[...]
     up = jnp.left_shift(jnp.int32(1), -exps).astype(jnp.float32)
     down = jnp.left_shift(jnp.int32(1), exps + 7).astype(jnp.float32) * (2.0**-7)
@@ -70,6 +86,7 @@
         kv_copies.append(c)
     kv_all[core, y, x, 0] = kv_send[z]
 
+    loads[5].wait()
     for g in range(HEADS // 2):
         pair = q_ref[:, 16 * g : 16 * g + 16, :].astype(jnp.float32)
         for i in range(2):
@@ -86,24 +103,56 @@
         q_copies.append(c)
     q_all[0] = q_send[z]
 
+    for c in loads[6:]:
+        c.wait()
+    nth = lax.broadcasted_iota(jnp.int32, (64, BLOCKS), 0) * 4
+    at_pos = lax.broadcasted_iota(jnp.int32, (64, BLOCKS), 1)
+    found = jnp.zeros((64, BLOCKS), jnp.int32)
+    for u in range(4):
+        b = nth + u
+        home = ((b >> 3) & 1) * 128 + ((b >> 1) & 3) * 32 + (b & 1) * 16 + ((b >> 4) & 1) * 8
+        home = home + (((b >> 5) - z) & 7)
+        here = jnp.broadcast_to(place_v[:, 32 * u : 32 * u + 1] >> 5, (64, BLOCKS))
+        found = found + jnp.where(here == at_pos, home, 0)
+    order_v[...] = jnp.sum(found, axis=0, keepdims=True) & (BLOCKS - 1)
+    to_scalar = pltpu.make_async_copy(order_v, order, ins.at[9])
+    to_scalar.start()
+
     def block_at(o):
-        return block_pos[lax.rem(z + o, 8) * 32 + (x % 2) * 16 + core * 8 + y * 2 + x // 2]
-
-    def starts(o, carry):
-        base = block_at(o) * TOK
-        pos = base + lax.broadcasted_iota(jnp.int32, (TOK * GROUP, DIM), 0) // GROUP
-        first = jnp.zeros((TOK * GROUP, DIM), jnp.int32)
-        end = jnp.int32(0)
-        for d in range(15):
-            end = end + doc_lengths[d]
-            first = jnp.where(pos >= end, end, first)
-        thr[o] = first - (base - REACH * TOK)
+        b = lax.rem(z + o, 8) * 32 + (x % 2) * 16 + core * 8 + y * 2 + x // 2
+        return place_s[b // 4, (b % 4) * 32] >> 5
+
+    channel = lax.broadcasted_iota(jnp.int32, (8, DIM), 1)
+    low = jnp.full((8, DIM), 1 << 20, jnp.int32)
+    high = low
+    end = jnp.int32(0)
+    for d in range(DOCS):
+        low = jnp.where(channel == d, end, low)
+        end = end + docs_s[d]
+        high = jnp.where(channel == d, end, high)
+    low, high = low[:1], high[:1]
+    step = lax.broadcasted_iota(jnp.int32, (N_ROWS, DIM), 0)
+
+    def key_docs(i, carry):
+        pos = step + (i - REACH * TOK // N_ROWS) * N_ROWS
+        at = pl.ds(i * 8, 8)
+        mask = jnp.where((pos >= low) & (pos < high), 0.0, -BIG).astype(jnp.bfloat16)
+        keys[at, :, pl.ds(DIM, DIM)] = mask.reshape(8, TOK, DIM)
+        vals[at, :, pl.ds(DIM, DIM)] = jnp.ones((8, TOK, DIM), jnp.bfloat16)
         return carry
 
-    lax.fori_loop(0, 8, starts, 0)
-    vwin[:, DIM:] = jnp.ones((PAD, DIM), jnp.bfloat16)
-    vwin[WIN:, :DIM] = jnp.zeros((PAD - WIN, DIM), jnp.bfloat16)
-    kwin[WIN:] = jnp.zeros((PAD - WIN, DIM), jnp.bfloat16)
+    lax.fori_loop(0, SORTED * TOK // N_ROWS, key_docs, 0)
+
+    def query_docs(o, carry):
+        pos = block_at(o) * TOK + step // GROUP
+        q_doc[o] = jnp.where((pos >= low) & (pos < high), 1.0, 0.0).astype(jnp.bfloat16)
+        return carry
+
+    lax.fori_loop(0, 8, query_docs, 0)
+    for ref in (keys, vals):
+        ref[:REACH, :, :DIM] = jnp.zeros((REACH, TOK, DIM), jnp.bfloat16)
+        ref[REACH + BLOCKS :, :, :DIM] = jnp.zeros((8, TOK, DIM), jnp.bfloat16)
+    to_scalar.wait()
 
     for c in kv_copies:
         c.wait_recv()
@@ -183,48 +232,54 @@
     for c in q_copies:
         c.wait_recv()
 
-    lane = lax.broadcasted_iota(jnp.int32, (TOK * GROUP, DIM), 1)
-    row = lax.broadcasted_iota(jnp.int32, (TOK * GROUP, DIM), 0)
-    causal = lane <= row // GROUP
+    def sort(i, carry):
+        for u in range(16):
+            p = i * 16 + u
+            b = order[0, p]
+            spot_of = (b >> 7, (b >> 5) & 3, (b >> 3) & 3, b & 7)
+            keys[p + REACH, :, pl.ds(0, DIM)] = kv_all[*spot_of, 0]
+            vals[p + REACH, :, pl.ds(0, DIM)] = kv_all[*spot_of, 1]
+        return carry
+
+    lax.fori_loop(0, BLOCKS // 16, sort, 0)
+
+    lane = lax.broadcasted_iota(jnp.int32, (N_ROWS, DIM), 1)
+    causal = lane <= step // GROUP
 
     def attend(j, carry):
         half, odd = j // 2, j % 2
         o = 4 + half - odd * (1 + 2 * half)
-        pos = block_at(o)
-
-        def fetch(i, c):
-            for u in range(5):
-                b = order[pos + i * 5 + u]
-                src = kv_all.at[b // 128, (b // 32) % 4, (b // 8) % 4, b % 8]
-                at = pl.ds(pl.multiple_of((i * 5 + u) * TOK, TOK), TOK)
-                kwin[at, :] = src[0]
-                vwin[at, pl.ds(0, DIM)] = src[1]
-            return c
-
-        lax.fori_loop(0, (REACH + 1) // 5, fetch, 0)
-        q = q_all[o]
-        first = thr[o]
-        top = jnp.full((TOK * GROUP, DIM), LOW, jnp.float32)
+        start = block_at(o)
+
+        def window(ref, c0, width):
+            blocks = ref[pl.ds(start + c0 // TOK, width // TOK)]
+            return blocks.reshape(width, 2 * DIM)
+
+        q = jnp.concatenate([q_all[o], q_doc[o]], axis=1)
+        top = jnp.full((N_ROWS, DIM), LOW, jnp.float32)
         for c0 in range(0, PAD, CHUNK):
             width = min(CHUNK, PAD - c0)
             s = lax.dot_general(
-                q, kwin[c0 : c0 + width, :], (((1,), (1,)), ((), ())),
+                q, window(keys, c0, width), (((1,), (1,)), ((), ())),
                 preferred_element_type=jnp.float32,
             )
             for t in range(0, width, DIM):
-                ok = lane + (c0 + t) >= first
+                tile = s[:, t : t + DIM]
                 if c0 + t == REACH * TOK:
-                    ok = ok & causal
-                tile = jnp.where(ok, s[:, t : t + DIM], LOW)
+                    tile = jnp.where(causal, tile, LOW)
                 scores[:, c0 + t : c0 + t + DIM] = tile
                 top = jnp.maximum(top, tile)
-        peak = jnp.max(top, axis=1, keepdims=True)
-        total = jnp.zeros((TOK * GROUP, 2 * DIM), jnp.float32)
+        peak = jnp.broadcast_to(jnp.max(top, axis=1, keepdims=True), (N_ROWS, DIM))
+        total = jnp.zeros((N_ROWS, 2 * DIM), jnp.float32)
         for c0 in range(0, PAD, CHUNK):
             width = min(CHUNK, PAD - c0)
-            w = jnp.exp2((scores[:, c0 : c0 + width] - peak) * FACTOR).astype(jnp.bfloat16)
+            tiles = [
+                jnp.exp2((scores[:, c0 + t : c0 + t + DIM] - peak) * FACTOR).astype(jnp.bfloat16)
+                for t in range(0, width, DIM)
+            ]
+            w = jnp.concatenate(tiles, axis=1)
             total = total + jnp.dot(
-                w, vwin[c0 : c0 + width, :], preferred_element_type=jnp.float32
+                w, window(vals, c0, width), preferred_element_type=jnp.float32
             )
         result = (total[:, :DIM] / total[:, DIM:]).astype(jnp.bfloat16)
         o_send[o] = result
@@ -260,46 +315,48 @@
 
 
 def shards(queries, keys, values, offsets, smooth_exp, scale_exp, placement, doc_lengths):
-    z = lax.axis_index("ctx") // 4
-    block_pos = placement.reshape(BLOCKS, TOK)[:, 0] // TOK
-    b = jnp.arange(BLOCKS, dtype=jnp.int32)
-    ctx, kv = b // 8, b % 8
-    x = (kv % 2) * 2 + (ctx // 2) % 2
-    place = (((ctx % 2) * 4 + kv // 2) * 4 + x) * 8 + (ctx // 4 - z) % 8
-    order = jnp.sum(
-        jnp.where(block_pos[None, :] == b[:, None], place[None, :], 0), axis=1
-    ).astype(jnp.int32)
-    order = jnp.concatenate([jnp.zeros((REACH,), jnp.int32), order])
     bf, f32 = jnp.bfloat16, jnp.float32
     dma = pltpu.SemaphoreType.DMA
-    smem = pl.BlockSpec(memory_space=pltpu.SMEM)
-    vmem = pl.BlockSpec(memory_space=pltpu.VMEM)
-    n_rows = TOK * GROUP
+    hbm = pl.BlockSpec(memory_space=pltpu.HBM)
     return pl.pallas_call(
         kernel,
-        out_shape=jax.ShapeDtypeStruct(queries.shape, bf),
-        in_specs=[smem] * 3 + [vmem] * 6,
-        out_specs=vmem,
+        out_shape=pltpu.VMEM(queries.shape, bf),
+        in_specs=[hbm] * 8,
+        out_specs=pl.BlockSpec(memory_space=pltpu.VMEM),
         scratch_shapes=[
+            pltpu.VMEM((64, DIM), jnp.int32),
+            pltpu.SMEM((64, DIM), jnp.int32),
+            pltpu.SMEM((DOCS,), jnp.int32),
+            pltpu.VMEM(queries.shape, bf),
+            pltpu.VMEM(keys.shape, bf),
+            pltpu.VMEM(values.shape, bf),
+            pltpu.VMEM(offsets.shape, jnp.int32),
+            pltpu.VMEM((HEADS, DIM), jnp.int32),
+            pltpu.VMEM((HEADS, DIM), jnp.int32),
+            pltpu.VMEM((1, BLOCKS), jnp.int32),
+            pltpu.SMEM((1, BLOCKS), jnp.int32),
             pltpu.VMEM((2, TOK * HEADS, DIM), f32),
             pltpu.VMEM((HEADS, 2, TOK, DIM), bf),
             pltpu.VMEM((2, 4, 4, 8, 2, TOK, DIM), bf),
-            pltpu.VMEM((HEADS, n_rows, DIM), bf),
-            pltpu.VMEM((8, n_rows, DIM), bf),
-            pltpu.VMEM((8, n_rows, DIM), bf),
-            pltpu.VMEM((HEADS, n_rows, DIM), bf),
-            pltpu.VMEM((8, n_rows, DIM), jnp.int32),
-            pltpu.VMEM((PAD, DIM), bf),
-            pltpu.VMEM((PAD, 2 * DIM), bf),
-            pltpu.VMEM((n_rows, PAD), f32),
+            pltpu.VMEM((HEADS, N_ROWS, DIM), bf),
+            pltpu.VMEM((8, N_ROWS, DIM), bf),
+            pltpu.VMEM((8, N_ROWS, DIM), bf),
+            pltpu.VMEM((8, N_ROWS, DIM), bf),
+            pltpu.VMEM((HEADS, N_ROWS, DIM), bf),
+            pltpu.VMEM((SORTED, TOK, 2 * DIM), bf),
+            pltpu.VMEM((SORTED, TOK, 2 * DIM), bf),
+            pltpu.VMEM((N_ROWS, PAD), f32),
             dma((8,)), dma((8,)), dma((8,)), dma((8,)), dma((8,)), dma((8,)),
-            dma((48,)), dma((48,)),
+            dma((48,)), dma((48,)), dma((10,)),
         ],
         compiler_params=pltpu.CompilerParams(
-            collective_id=0, has_side_effects=True, vmem_limit_bytes=40 * 2**20
+            collective_id=0, has_side_effects=True, vmem_limit_bytes=60 * 2**20
         ),
         name="attend",
-    )(order, block_pos, doc_lengths, queries, keys, values, offsets, smooth_exp, scale_exp)
+    )(
+        placement.reshape(64, DIM), doc_lengths, queries, keys, values, offsets, smooth_exp,
+        scale_exp,
+    )
 
 
 def solution(mesh):

time: 69 us -> 56.1 us (0.81)
  Pallas kernels: 65.2 us -> 55.3 us
  local copies, waits for them, and re-layouts: 3.38 us -> 0.8 us
    pallas_call x1, Pallas kernels: 65.2 us -> 55.3 us  [shards(): pl.pallas_call(kernel, out_shape=pltpu.VMEM(queries.shape, bf), in_specs=...]
    unnamed x17 -> x1, local copies, waits for them, and re-layouts: 3.12 us -> 0.8 us
where the time goes in v2:
time: 56.1 us
  Pallas kernels  55.3 us (99%)
  local copies, waits for them, and re-layouts  0.8 us (1%)
    pallas_call x1, Pallas kernels, shards(): pl.pallas_call(kernel, out_shape=pltpu.VMEM(queries.shape, bf), in_specs=...  55.3 us

profile of v2, /device:TPU:1, one launch (start us, length us, event | category | flops | bytes accessed | tf_op | source)
XLA Modules:
  0.0 56.1 jit_solution(17715063059830333074)
XLA Ops:
  0.0 55.3 %attend.1 = bf16[32,64,128]{2,1,0:T(8,128)(2,1)S(1)} custom-call(s32[64,128]{1,0:T(8,128)} %bitcast.1, s32[16]{0:T(128)} %docs_hbm.1, bf16[32,64,128]{2,1,0:T(8,128)(2,1)} %q_hbm.1, bf16[32,8,128]{2,1,0:T(8,128)(2,1)} %k_hbm.1, bf16[32,8,128]{2,1,0:T(8,128)(2,1)} %v_hbm.1, s32[32,8,128]{2,1,0:T(8,128)} %off_hbm.1, s32[8,128]{1,0:T(8,128)} %smooth_hbm.1, ...), custom_call_target="tpu_custom_call" | custom-call | tf_op jit(solution)/shard_map/attend/pallas_call | solution.py:321
  55.3 0.8 %copy.10 = bf16[32,64,128]{2,1,0:T(8,128)(2,1)} copy(bf16[32,64,128]{2,1,0:T(8,128)(2,1)S(1)} %attend.1) | data formatting | bytes 1048576

commit v3 on v2

--- a/solution.py
+++ b/solution.py
@@ -29,7 +29,7 @@
 def kernel(
     place_hbm, docs_hbm, q_hbm, k_hbm, v_hbm, off_hbm, smooth_hbm, scale_hbm, out_ref,
     place_v, place_s, docs_s, q_ref, k_ref, v_ref, off_ref, smooth_ref, scale_ref, order_v, order,
-    rows, kv_send, kv_all, q_send, q_all, q_doc, o_send, o_all, keys, vals, scores,
+    rows, kv_send, kv_all, q_send, q_all, q_doc, o_send, o_all, keys, vals, scores, peaks,
     kvs, kvr, qs, qr, os, orr, gs, gr, ins,
 ):
     loads = []
@@ -50,10 +50,10 @@
     def along_z(o):
         return spot(x, y, lax.rem(z + o, 8), core)
 
-    x_next = [spot((x + d) % 4, y, z, core) for d in (1, 3)]
-    y_next = [spot(x, (y + d) % 4, z, core) for d in (1, 3)]
+    along_x = [spot((x + d) % 4, y, z, core) for d in range(4)]
+    along_y = [spot(x, (y + d) % 4, z, core) for d in range(4)]
     twin = spot(x, y, z, 1 - core)
-    greeted = [along_z(o) for o in range(1, 8)] + x_next + y_next + [twin]
+    greeted = [along_z(o) for o in range(1, 8)] + along_x[1:] + along_y[1:] + [twin]
     barrier = pltpu.get_barrier_semaphore()
     for peer in greeted:
         pl.semaphore_signal(barrier, inc=1, device_id=peer, device_id_type=MESH)
@@ -75,16 +75,18 @@
 
     pl.semaphore_wait(barrier, len(greeted))
 
+    line, other = (y, x), (x, y)
     far_first = (4, 3, 5, 2, 6, 1, 7)
     kv_copies = []
     for o in far_first:
         c = pltpu.make_async_remote_copy(
-            kv_send.at[lax.rem(z + o, 8)], kv_all.at[core, y, x, 8 - o],
+            kv_send.at[lax.rem(z + o, 8)],
+            kv_all.at[(8 - o) // 4, core, line[(8 - o) // 4], 0, (8 - o) % 4],
             kvs.at[o], kvr.at[8 - o], device_id=along_z(o), device_id_type=MESH,
         )
         c.start()
         kv_copies.append(c)
-    kv_all[core, y, x, 0] = kv_send[z]
+    kv_all[0, core, y, 0, 0] = kv_send[z]
 
     loads[5].wait()
     for g in range(HEADS // 2):
@@ -110,8 +112,11 @@
     found = jnp.zeros((64, BLOCKS), jnp.int32)
     for u in range(4):
         b = nth + u
-        home = ((b >> 3) & 1) * 128 + ((b >> 1) & 3) * 32 + (b & 1) * 16 + ((b >> 4) & 1) * 8
-        home = home + (((b >> 5) - z) & 7)
+        their_x, their_y = (b & 1) * 2 + ((b >> 4) & 1), (b >> 1) & 3
+        deep = ((b >> 5) - z) & 7
+        first = their_y * 16 + ((their_x - x) & 3) * 4 + deep
+        second = their_x * 16 + ((their_y - y) & 3) * 4 + deep + 124
+        home = ((b >> 3) & 1) * 64 + jnp.where(deep < 4, first, second)
         here = jnp.broadcast_to(place_v[:, 32 * u : 32 * u + 1] >> 5, (64, BLOCKS))
         found = found + jnp.where(here == at_pos, home, 0)
     order_v[...] = jnp.sum(found, axis=0, keepdims=True) & (BLOCKS - 1)
@@ -154,80 +159,68 @@
         ref[REACH + BLOCKS :, :, :DIM] = jnp.zeros((8, TOK, DIM), jnp.bfloat16)
     to_scalar.wait()
 
-    for c in kv_copies:
-        c.wait_recv()
-
     sends = []
 
-    def send(ref, target):
+    def send(src, dst, target):
         i = len(sends)
         c = pltpu.make_async_remote_copy(
-            ref, ref, gs.at[i], gr.at[i], device_id=target, device_id_type=MESH
+            src, dst, gs.at[i], gr.at[i], device_id=target, device_id_type=MESH
         )
         c.start()
         sends.append(c)
         return c
 
-    nexts = {"x": x_next, "y": y_next}
-    parts = (("x", "y", 0), ("y", "x", 4))
-
-    def piece(rel, lo, n):
-        return kv_all.at[core, (y + rel[1] + 4) % 4, (x + rel[0] + 4) % 4, pl.ds(lo, n)]
-
-    def both(axis, rel, lo):
-        return [send(piece(rel, lo, 4), target) for target in nexts[axis]]
-
-    def moved(rel, axis, d):
-        return (rel[0] + d, rel[1]) if axis == "x" else (rel[0], rel[1] + d)
-
-    def pass_on(axis, rel, lo, copies):
+    arrived = dict(zip(far_first, kv_copies))
+    inner, outer = (along_x, along_y), (along_y, along_x)
+    own, others, whole = pl.ds(0, 1), pl.ds(1, 3), pl.ds(0, 4)
+
+    def row(p, d, columns, depth=whole):
+        return kv_all.at[p, core, (line[p] + d) % 4, columns, depth]
+
+    def same(ref, target):
+        return send(ref, ref, target)
+
+    def spread(p, columns):
+        return [same(row(p, 0, columns), outer[p][d]) for d in (1, 3)]
+
+    def pass_on(p, columns, copies):
         copies[0].wait_recv()
-        a = send(piece(moved(rel, axis, -1), lo, 2), nexts[axis][0])
+        a = same(row(p, 3, columns, pl.ds(0, 2)), outer[p][1])
         copies[1].wait_recv()
-        b = send(piece(moved(rel, axis, 1), lo + 2, 2), nexts[axis][1])
+        b = same(row(p, 1, columns, pl.ds(2, 2)), outer[p][3])
         return [a, b]
 
-    twin_copies = []
-
-    def line_to_twin(second, rel, lo):
-        if second == "y":
-            ref = kv_all.at[core, :, (x + rel[0] + 4) % 4, pl.ds(lo, 4)]
-        else:
-            ref = kv_all.at[core, (y + rel[1] + 4) % 4, :, pl.ds(lo, 4)]
-        twin_copies.append(send(ref, twin))
-
-    one = [both(p[0], (0, 0), p[2]) for p in parts]
-    two = [(p, (0, 0), both(p[1], (0, 0), p[2])) for p in parts]
-    opposite = [pass_on(p[0], (0, 0), p[2], c) for p, c in zip(parts, one)]
-    for d in (-1, 1):
-        for p in parts:
-            rel = moved((0, 0), p[0], d)
-            two.append((p, rel, both(p[1], rel, p[2])))
-    last = []
-
-    def second(entry):
-        p, rel, copies = entry
-        last.append((p, rel, pass_on(p[1], rel, p[2], copies)))
-
-    def finish(entry):
-        p, rel, copies = entry
-        for c in copies:
+    def to_twin(p, d):
+        return same(row(p, d, whole), twin)
+
+    rows_in, own_in, others_in, twin_in = [], [], [], []
+    for p in range(2):
+        for o in far_first:
+            if (8 - o) // 4 == p:
+                arrived[o].wait_recv()
+        rows_in.append(
+            [
+                send(row(p, 0, own), kv_all.at[p, core, line[p], pl.ds(4 - d, 1)], inner[p][d])
+                for d in (2, 1, 3)
+            ]
+        )
+    for p in range(2):
+        own_in.append(spread(p, own))
+    for p in range(2):
+        for c in rows_in[p]:
             c.wait_recv()
-        line_to_twin(p[1], rel, p[2])
-
-    second(two[0])
-    second(two[1])
-    for p, copies in zip(parts, opposite):
-        for c in copies:
+        others_in.append(spread(p, others))
+        twin_in.append(to_twin(p, 0))
+    last = [pass_on(p, own, own_in[p]) for p in range(2)]
+    for p in range(2):
+        last[p] = last[p] + pass_on(p, others, others_in[p])
+        twin_in.append(to_twin(p, 3))
+        twin_in.append(to_twin(p, 1))
+    for p in range(2):
+        for c in last[p]:
             c.wait_recv()
-        rel = moved((0, 0), p[0], 2)
-        two.append((p, rel, both(p[1], rel, p[2])))
-    for i in range(2, len(two)):
-        second(two[i])
-        finish(last[i - 2])
-    for entry in last[len(two) - 2 :]:
-        finish(entry)
-    for c in twin_copies:
+        twin_in.append(to_twin(p, 2))
+    for c in twin_in:
         c.wait_recv()
     for c in q_copies:
         c.wait_recv()
@@ -236,7 +229,7 @@
         for u in range(16):
             p = i * 16 + u
             b = order[0, p]
-            spot_of = (b >> 7, (b >> 5) & 3, (b >> 3) & 3, b & 7)
+            spot_of = (b >> 7, (b >> 6) & 1, (b >> 4) & 3, (b >> 2) & 3, b & 3)
             keys[p + REACH, :, pl.ds(0, DIM)] = kv_all[*spot_of, 0]
             vals[p + REACH, :, pl.ds(0, DIM)] = kv_all[*spot_of, 1]
         return carry
@@ -246,60 +239,69 @@
     lane = lax.broadcasted_iota(jnp.int32, (N_ROWS, DIM), 1)
     causal = lane <= step // GROUP
 
-    def attend(j, carry):
-        half, odd = j // 2, j % 2
-        o = 4 + half - odd * (1 + 2 * half)
-        start = block_at(o)
-
-        def window(ref, c0, width):
-            blocks = ref[pl.ds(start + c0 // TOK, width // TOK)]
-            return blocks.reshape(width, 2 * DIM)
-
+    def window(ref, o, c0, width):
+        blocks = ref[pl.ds(block_at(o) + c0 // TOK, width // TOK)]
+        return blocks.reshape(width, 2 * DIM)
+
+    def score(o, slot):
         q = jnp.concatenate([q_all[o], q_doc[o]], axis=1)
         top = jnp.full((N_ROWS, DIM), LOW, jnp.float32)
         for c0 in range(0, PAD, CHUNK):
             width = min(CHUNK, PAD - c0)
             s = lax.dot_general(
-                q, window(keys, c0, width), (((1,), (1,)), ((), ())),
+                q, window(keys, o, c0, width), (((1,), (1,)), ((), ())),
                 preferred_element_type=jnp.float32,
             )
             for t in range(0, width, DIM):
                 tile = s[:, t : t + DIM]
                 if c0 + t == REACH * TOK:
                     tile = jnp.where(causal, tile, LOW)
-                scores[:, c0 + t : c0 + t + DIM] = tile
+                scores[slot, :, c0 + t : c0 + t + DIM] = tile
                 top = jnp.maximum(top, tile)
-        peak = jnp.broadcast_to(jnp.max(top, axis=1, keepdims=True), (N_ROWS, DIM))
+        peaks[slot] = jnp.broadcast_to(jnp.max(top, axis=1, keepdims=True), (N_ROWS, DIM))
+
+    def weigh(o, slot, peak):
         total = jnp.zeros((N_ROWS, 2 * DIM), jnp.float32)
         for c0 in range(0, PAD, CHUNK):
             width = min(CHUNK, PAD - c0)
             tiles = [
-                jnp.exp2((scores[:, c0 + t : c0 + t + DIM] - peak) * FACTOR).astype(jnp.bfloat16)
+                jnp.exp2((scores[slot, :, c0 + t : c0 + t + DIM] - peak) * FACTOR)
                 for t in range(0, width, DIM)
             ]
-            w = jnp.concatenate(tiles, axis=1)
+            w = jnp.concatenate([tile.astype(jnp.bfloat16) for tile in tiles], axis=1)
             total = total + jnp.dot(
-                w, window(vals, c0, width), preferred_element_type=jnp.float32
+                w, window(vals, o, c0, width), preferred_element_type=jnp.float32
             )
-        result = (total[:, :DIM] / total[:, DIM:]).astype(jnp.bfloat16)
-        o_send[o] = result
-
-        @pl.when(j < 7)
-        def _():
-            pltpu.make_async_remote_copy(
-                o_send.at[o], o_all.at[z], os.at[o], orr.at[lax.rem(8 - o, 8)],
-                device_id=along_z(o), device_id_type=MESH,
-            ).start()
-
+        o_send[o] = (total[:, :DIM] / total[:, DIM:]).astype(jnp.bfloat16)
+
+    def home_copy(o):
+        return pltpu.make_async_remote_copy(
+            o_send.at[o], o_all.at[z], os.at[o], orr.at[lax.rem(8 - o, 8)],
+            device_id=along_z(o), device_id_type=MESH,
+        )
+
+    score(4, 0)
+
+    def two(i, carry):
+        peak = peaks[0]
+        score(3 - i, 1)
+        weigh(4 + i, 0, peak)
+        home_copy(4 + i).start()
+        peak = peaks[1]
+        score(5 + i, 0)
+        weigh(3 - i, 1, peak)
+        home_copy(3 - i).start()
         return carry
 
-    lax.fori_loop(0, 8, attend, 0)
+    lax.fori_loop(0, 3, two, 0)
+    peak = peaks[0]
+    score(0, 1)
+    weigh(7, 0, peak)
+    home_copy(7).start()
+    weigh(0, 1, peaks[1])
     o_all[z] = o_send[0]
     for o in far_first:
-        pltpu.make_async_remote_copy(
-            o_send.at[o], o_all.at[z], os.at[o], orr.at[8 - o],
-            device_id=along_z(o), device_id_type=MESH,
-        ).wait_recv()
+        home_copy(o).wait_recv()
     for g in range(HEADS // 2):
         pair = [
             o_all[2 * g + i].astype(jnp.float32).reshape(TOK, GROUP, DIM) for i in range(2)
@@ -308,10 +310,7 @@
     for c in kv_copies + q_copies + sends:
         c.wait_send()
     for o in far_first:
-        pltpu.make_async_remote_copy(
-            o_send.at[o], o_all.at[z], os.at[o], orr.at[8 - o],
-            device_id=along_z(o), device_id_type=MESH,
-        ).wait_send()
+        home_copy(o).wait_send()
 
 
 def shards(queries, keys, values, offsets, smooth_exp, scale_exp, placement, doc_lengths):
@@ -337,7 +336,7 @@
             pltpu.SMEM((1, BLOCKS), jnp.int32),
             pltpu.VMEM((2, TOK * HEADS, DIM), f32),
             pltpu.VMEM((HEADS, 2, TOK, DIM), bf),
-            pltpu.VMEM((2, 4, 4, 8, 2, TOK, DIM), bf),
+            pltpu.VMEM((2, 2, 4, 4, 4, 2, TOK, DIM), bf),
             pltpu.VMEM((HEADS, N_ROWS, DIM), bf),
             pltpu.VMEM((8, N_ROWS, DIM), bf),
             pltpu.VMEM((8, N_ROWS, DIM), bf),
@@ -345,9 +344,10 @@
             pltpu.VMEM((HEADS, N_ROWS, DIM), bf),
             pltpu.VMEM((SORTED, TOK, 2 * DIM), bf),
             pltpu.VMEM((SORTED, TOK, 2 * DIM), bf),
-            pltpu.VMEM((N_ROWS, PAD), f32),
+            pltpu.VMEM((2, N_ROWS, PAD), f32),
+            pltpu.VMEM((2, N_ROWS, DIM), f32),
             dma((8,)), dma((8,)), dma((8,)), dma((8,)), dma((8,)), dma((8,)),
-            dma((48,)), dma((48,)), dma((10,)),
+            dma((30,)), dma((30,)), dma((10,)),
         ],
         compiler_params=pltpu.CompilerParams(
             collective_id=0, has_side_effects=True, vmem_limit_bytes=60 * 2**20

time: 56.1 us -> 53 us (0.945)
  Pallas kernels: 55.3 us -> 52.1 us
    pallas_call x1, Pallas kernels: 55.3 us -> 52.1 us  [shards(): pl.pallas_call(kernel, out_shape=pltpu.VMEM(queries.shape, bf), in_specs=...]
where the time goes in v3:
time: 53 us; the launch traced here: 52.9 us
  Pallas kernels  52.1 us (98%)
  local copies, waits for them, and re-layouts  0.8 us (2%)
    pallas_call x1, Pallas kernels, shards(): pl.pallas_call(kernel, out_shape=pltpu.VMEM(queries.shape, bf), in_specs=...  52.1 us

profile of v3, /device:TPU:1, one launch (start us, length us, event | category | flops | bytes accessed | tf_op | source)
XLA Modules:
  0.0 52.9 jit_solution(17181381584696935851)
XLA Ops:
  0.0 52.1 %attend.1 = bf16[32,64,128]{2,1,0:T(8,128)(2,1)S(1)} custom-call(s32[64,128]{1,0:T(8,128)} %bitcast.1, s32[16]{0:T(128)} %docs_hbm.1, bf16[32,64,128]{2,1,0:T(8,128)(2,1)} %q_hbm.1, bf16[32,8,128]{2,1,0:T(8,128)(2,1)} %k_hbm.1, bf16[32,8,128]{2,1,0:T(8,128)(2,1)} %v_hbm.1, s32[32,8,128]{2,1,0:T(8,128)} %off_hbm.1, s32[8,128]{1,0:T(8,128)} %smooth_hbm.1, ...), custom_call_target="tpu_custom_call" | custom-call | tf_op jit(solution)/shard_map/attend/pallas_call | solution.py:320
  52.2 0.8 %copy.10 = bf16[32,64,128]{2,1,0:T(8,128)(2,1)} copy(bf16[32,64,128]{2,1,0:T(8,128)(2,1)S(1)} %attend.1) | data formatting | bytes 1048576

commit v4 on v3

--- a/solution.py
+++ b/solution.py
@@ -32,6 +32,24 @@
     rows, kv_send, kv_all, q_send, q_all, q_doc, o_send, o_all, keys, vals, scores, peaks,
     kvs, kvr, qs, qr, os, orr, gs, gr, ins,
 ):
+    kv = lax.axis_index("kv")
+    ctx = lax.axis_index("ctx")
+    y, z, core = kv // 2, ctx // 4, ctx % 2
+    x = (kv % 2) * 2 + (ctx // 2) % 2
+
+    def along_z(o):
+        return spot(x, y, lax.rem(z + o, 8), core)
+
+    line = y * (1 - core) + x * core
+    inner = [spot((x + d * (1 - core)) % 4, (y + d * core) % 4, z, core) for d in range(4)]
+    outer = [spot((x + d * core) % 4, (y + d * (1 - core)) % 4, z, core) for d in range(4)]
+    twin = spot(x, y, z, 1 - core)
+    greeted = [along_z(o) for o in range(1, 8)] + inner[1:] + outer[1:] + [twin]
+    greeted = greeted + [spot(x, y, lax.rem(z + o, 8), 1 - core) for o in range(1, 8)]
+    barrier = pltpu.get_barrier_semaphore()
+    for peer in greeted:
+        pl.semaphore_signal(barrier, inc=1, device_id=peer, device_id_type=MESH)
+
     loads = []
     pairs = (
         (k_hbm, k_ref), (off_hbm, off_ref), (smooth_hbm, smooth_ref), (scale_hbm, scale_ref),
@@ -42,22 +60,6 @@
         c = pltpu.make_async_copy(src, dst, ins.at[i])
         c.start()
         loads.append(c)
-    kv = lax.axis_index("kv")
-    ctx = lax.axis_index("ctx")
-    y, z, core = kv // 2, ctx // 4, ctx % 2
-    x = (kv % 2) * 2 + (ctx // 2) % 2
-
-    def along_z(o):
-        return spot(x, y, lax.rem(z + o, 8), core)
-
-    along_x = [spot((x + d) % 4, y, z, core) for d in range(4)]
-    along_y = [spot(x, (y + d) % 4, z, core) for d in range(4)]
-    twin = spot(x, y, z, 1 - core)
-    greeted = [along_z(o) for o in range(1, 8)] + along_x[1:] + along_y[1:] + [twin]
-    barrier = pltpu.get_barrier_semaphore()
-    for peer in greeted:
-        pl.semaphore_signal(barrier, inc=1, device_id=peer, device_id_type=MESH)
-
     for c in loads[:5]:
         c.wait()
     exps = smooth_ref[...] + scale_ref[...]
@@ -75,18 +77,30 @@
 
     pl.semaphore_wait(barrier, len(greeted))
 
-    line, other = (y, x), (x, y)
     far_first = (4, 3, 5, 2, 6, 1, 7)
-    kv_copies = []
-    for o in far_first:
+    kv_copies = {}
+    for o in (7, 1, 6, 2, 5, 3, 4):
+        to, n = (1, o - 1) if o < 5 else (0, 8 - o)
+        there = y if to == 0 else x
         c = pltpu.make_async_remote_copy(
-            kv_send.at[lax.rem(z + o, 8)],
-            kv_all.at[(8 - o) // 4, core, line[(8 - o) // 4], 0, (8 - o) % 4],
-            kvs.at[o], kvr.at[8 - o], device_id=along_z(o), device_id_type=MESH,
+            kv_send.at[lax.rem(z + o, 8)], kv_all.at[to, there, 0, n, core],
+            kvs.at[o], kvr.at[n, core],
+            device_id=spot(x, y, lax.rem(z + o, 8), to), device_id_type=MESH,
         )
         c.start()
-        kv_copies.append(c)
-    kv_all[0, core, y, 0, 0] = kv_send[z]
+        kv_copies[o] = c
+    beside = pltpu.make_async_remote_copy(
+        kv_send.at[z], kv_all.at[0, y, 0, 0, 1], kvs.at[0], kvr.at[0, 1],
+        device_id=twin, device_id_type=MESH,
+    )
+
+    @pl.when(core == 0)
+    def _():
+        kv_all[0, y, 0, 0, 0] = kv_send[z]
+
+    @pl.when(core == 1)
+    def _():
+        beside.start()
 
     loads[5].wait()
     for g in range(HEADS // 2):
@@ -95,14 +109,6 @@
             q_send[2 * g + i] = (
                 pair[:, 8 * i : 8 * i + 8, :].reshape(TOK * GROUP, DIM).astype(jnp.bfloat16)
             )
-    q_copies = []
-    for o in far_first:
-        c = pltpu.make_async_remote_copy(
-            q_send.at[lax.rem(z + o, 8)], q_all.at[8 - o],
-            qs.at[o], qr.at[8 - o], device_id=along_z(o), device_id_type=MESH,
-        )
-        c.start()
-        q_copies.append(c)
     q_all[0] = q_send[z]
 
     for c in loads[6:]:
@@ -114,9 +120,9 @@
         b = nth + u
         their_x, their_y = (b & 1) * 2 + ((b >> 4) & 1), (b >> 1) & 3
         deep = ((b >> 5) - z) & 7
-        first = their_y * 16 + ((their_x - x) & 3) * 4 + deep
-        second = their_x * 16 + ((their_y - y) & 3) * 4 + deep + 124
-        home = ((b >> 3) & 1) * 64 + jnp.where(deep < 4, first, second)
+        first = (their_y * 4 + ((their_x - x) & 3)) * 4 + deep
+        second = (their_x * 4 + ((their_y - y) & 3)) * 4 + 71 - deep
+        home = jnp.where(deep < 4, first, second) * 2 + ((b >> 3) & 1)
         here = jnp.broadcast_to(place_v[:, 32 * u : 32 * u + 1] >> 5, (64, BLOCKS))
         found = found + jnp.where(here == at_pos, home, 0)
     order_v[...] = jnp.sum(found, axis=0, keepdims=True) & (BLOCKS - 1)
@@ -170,56 +176,83 @@
         sends.append(c)
         return c
 
-    arrived = dict(zip(far_first, kv_copies))
-    inner, outer = (along_x, along_y), (along_y, along_x)
-    own, others, whole = pl.ds(0, 1), pl.ds(1, 3), pl.ds(0, 4)
-
-    def row(p, d, columns, depth=whole):
-        return kv_all.at[p, core, (line[p] + d) % 4, columns, depth]
+    own, others, whole = (0, 1), (1, 3), (0, 4)
+
+    def row(i, d, columns, half=None):
+        ref = kv_all.at[core, (line + d) % 4, pl.ds(*columns), pl.ds(i, 1)]
+        return ref if half is None else ref.at[:, :, pl.ds(half, 1)]
 
     def same(ref, target):
         return send(ref, ref, target)
 
-    def spread(p, columns):
-        return [same(row(p, 0, columns), outer[p][d]) for d in (1, 3)]
-
-    def pass_on(p, columns, copies):
+    def spread(i, columns):
+        return [same(row(i, 0, columns), outer[d]) for d in (1, 3)]
+
+    def pass_on(i, columns, copies):
         copies[0].wait_recv()
-        a = same(row(p, 3, columns, pl.ds(0, 2)), outer[p][1])
+        a = same(row(i, 3, columns, 0), outer[1])
         copies[1].wait_recv()
-        b = same(row(p, 1, columns, pl.ds(2, 2)), outer[p][3])
+        b = same(row(i, 1, columns, 1), outer[3])
         return [a, b]
 
-    def to_twin(p, d):
-        return same(row(p, d, whole), twin)
-
-    rows_in, own_in, others_in, twin_in = [], [], [], []
-    for p in range(2):
-        for o in far_first:
-            if (8 - o) // 4 == p:
-                arrived[o].wait_recv()
+    def to_twin(i, d):
+        return same(row(i, d, whole), twin)
+
+    def arrive(n, c):
+        return pltpu.make_async_remote_copy(
+            kv_send.at[0], kv_all.at[core, line, 0, n, c], kvs.at[0], kvr.at[n, c],
+            device_id=twin, device_id_type=MESH,
+        )
+
+    rows_in, twin_in, own_in = [], [], []
+    for i in range(4):
+        for c in range(2):
+            if i or c:
+                arrive(i, c).wait_recv()
+            else:
+                pl.when(core == 1)(arrive(i, c).wait_recv)
         rows_in.append(
             [
-                send(row(p, 0, own), kv_all.at[p, core, line[p], pl.ds(4 - d, 1)], inner[p][d])
+                send(row(i, 0, own), row(i, 0, (4 - d, 1)), inner[d])
                 for d in (2, 1, 3)
             ]
         )
-    for p in range(2):
-        own_in.append(spread(p, own))
-    for p in range(2):
-        for c in rows_in[p]:
+        own_in.append(spread(i, own))
+    q_copies = []
+    for o in far_first:
+        c = pltpu.make_async_remote_copy(
+            q_send.at[lax.rem(z + o, 8)], q_all.at[8 - o],
+            qs.at[o], qr.at[8 - o], device_id=along_z(o), device_id_type=MESH,
+        )
+        c.start()
+        q_copies.append(c)
+    ring_in, last = [], []
+
+    def widen(i):
+        for c in rows_in[i]:
             c.wait_recv()
-        others_in.append(spread(p, others))
-        twin_in.append(to_twin(p, 0))
-    last = [pass_on(p, own, own_in[p]) for p in range(2)]
-    for p in range(2):
-        last[p] = last[p] + pass_on(p, others, others_in[p])
-        twin_in.append(to_twin(p, 3))
-        twin_in.append(to_twin(p, 1))
-    for p in range(2):
-        for c in last[p]:
+        ring_in.append(spread(i, others))
+        twin_in.append(to_twin(i, 0))
+        last.append([])
+
+    def turn(i):
+        last[i] += pass_on(i, others, ring_in[i])
+        twin_in.append(to_twin(i, 3))
+        twin_in.append(to_twin(i, 1))
+
+    def finish(i):
+        for c in last[i]:
             c.wait_recv()
-        twin_in.append(to_twin(p, 2))
+        twin_in.append(to_twin(i, 2))
+
+    for i in range(4):
+        widen(i)
+    for i in range(4):
+        last[i] += pass_on(i, own, own_in[i])
+    for i in range(4):
+        turn(i)
+    for i in range(4):
+        finish(i)
     for c in twin_in:
         c.wait_recv()
     for c in q_copies:
@@ -229,7 +262,7 @@
         for u in range(16):
             p = i * 16 + u
             b = order[0, p]
-            spot_of = (b >> 7, (b >> 6) & 1, (b >> 4) & 3, (b >> 2) & 3, b & 3)
+            spot_of = (b >> 7, (b >> 5) & 3, (b >> 3) & 3, (b >> 1) & 3, b & 1)
             keys[p + REACH, :, pl.ds(0, DIM)] = kv_all[*spot_of, 0]
             vals[p + REACH, :, pl.ds(0, DIM)] = kv_all[*spot_of, 1]
         return carry
@@ -307,7 +340,8 @@
             o_all[2 * g + i].astype(jnp.float32).reshape(TOK, GROUP, DIM) for i in range(2)
         ]
         out_ref[:, 16 * g : 16 * g + 16, :] = jnp.concatenate(pair, axis=1).astype(jnp.bfloat16)
-    for c in kv_copies + q_copies + sends:
+    pl.when(core == 1)(beside.wait_send)
+    for c in list(kv_copies.values()) + q_copies + sends:
         c.wait_send()
     for o in far_first:
         home_copy(o).wait_send()
@@ -336,7 +370,7 @@
             pltpu.SMEM((1, BLOCKS), jnp.int32),
             pltpu.VMEM((2, TOK * HEADS, DIM), f32),
             pltpu.VMEM((HEADS, 2, TOK, DIM), bf),
-            pltpu.VMEM((2, 2, 4, 4, 4, 2, TOK, DIM), bf),
+            pltpu.VMEM((2, 4, 4, 4, 2, 2, TOK, DIM), bf),
             pltpu.VMEM((HEADS, N_ROWS, DIM), bf),
             pltpu.VMEM((8, N_ROWS, DIM), bf),
             pltpu.VMEM((8, N_ROWS, DIM), bf),
@@ -346,8 +380,8 @@
             pltpu.VMEM((SORTED, TOK, 2 * DIM), bf),
             pltpu.VMEM((2, N_ROWS, PAD), f32),
             pltpu.VMEM((2, N_ROWS, DIM), f32),
-            dma((8,)), dma((8,)), dma((8,)), dma((8,)), dma((8,)), dma((8,)),
-            dma((30,)), dma((30,)), dma((10,)),
+            dma((8,)), dma((4, 2)), dma((8,)), dma((8,)), dma((8,)), dma((8,)),
+            dma((60,)), dma((60,)), dma((10,)),
         ],
         compiler_params=pltpu.CompilerParams(
             collective_id=0, has_side_effects=True, vmem_limit_bytes=60 * 2**20

time: 53 us -> 49.1 us (0.926)
  Pallas kernels: 52.1 us -> 48.2 us
    pallas_call x1, Pallas kernels: 52.1 us -> 48.2 us  [shards(): pl.pallas_call(kernel, out_shape=pltpu.VMEM(queries.shape, bf), in_specs=...]
where the time goes in v4:
time: 49.1 us; the launch traced here: 49 us
  Pallas kernels  48.2 us (98%)
  local copies, waits for them, and re-layouts  0.8 us (2%)
    pallas_call x1, Pallas kernels, shards(): pl.pallas_call(kernel, out_shape=pltpu.VMEM(queries.shape, bf), in_specs=...  48.2 us

profile of v4, /device:TPU:1, one launch (start us, length us, event | category | flops | bytes accessed | tf_op | source)
XLA Modules:
  0.0 49.0 jit_solution(6255222836527610701)
XLA Ops:
  0.0 48.2 %attend.1 = bf16[32,64,128]{2,1,0:T(8,128)(2,1)S(1)} custom-call(s32[64,128]{1,0:T(8,128)} %bitcast.1, s32[16]{0:T(128)} %docs_hbm.1, bf16[32,64,128]{2,1,0:T(8,128)(2,1)} %q_hbm.1, bf16[32,8,128]{2,1,0:T(8,128)(2,1)} %k_hbm.1, bf16[32,8,128]{2,1,0:T(8,128)(2,1)} %v_hbm.1, s32[32,8,128]{2,1,0:T(8,128)} %off_hbm.1, s32[8,128]{1,0:T(8,128)} %smooth_hbm.1, ...), custom_call_target="tpu_custom_call" | custom-call | tf_op jit(solution)/shard_map/attend/pallas_call | solution.py:354
  48.2 0.8 %copy.10 = bf16[32,64,128]{2,1,0:T(8,128)(2,1)} copy(bf16[32,64,128]{2,1,0:T(8,128)(2,1)S(1)} %attend.1) | data formatting | bytes 1048576

commit v5 on v4

--- a/solution.py
+++ b/solution.py
@@ -45,7 +45,8 @@
     outer = [spot((x + d * core) % 4, (y + d * (1 - core)) % 4, z, core) for d in range(4)]
     twin = spot(x, y, z, 1 - core)
     greeted = [along_z(o) for o in range(1, 8)] + inner[1:] + outer[1:] + [twin]
-    greeted = greeted + [spot(x, y, lax.rem(z + o, 8), 1 - core) for o in range(1, 8)]
+    cross = [lax.rem(z + k * (1 - 2 * core) + 8, 8) for k in range(1, 5)]
+    greeted = greeted + [spot(x, y, there, 1 - core) for there in cross]
     barrier = pltpu.get_barrier_semaphore()
     for peer in greeted:
         pl.semaphore_signal(barrier, inc=1, device_id=peer, device_id_type=MESH)
@@ -235,11 +236,6 @@
         twin_in.append(to_twin(i, 0))
         last.append([])
 
-    def turn(i):
-        last[i] += pass_on(i, others, ring_in[i])
-        twin_in.append(to_twin(i, 3))
-        twin_in.append(to_twin(i, 1))
-
     def finish(i):
         for c in last[i]:
             c.wait_recv()
@@ -250,7 +246,10 @@
     for i in range(4):
         last[i] += pass_on(i, own, own_in[i])
     for i in range(4):
-        turn(i)
+        last[i] += pass_on(i, others, ring_in[i])
+    for i in range(4):
+        twin_in.append(to_twin(i, 3))
+        twin_in.append(to_twin(i, 1))
     for i in range(4):
         finish(i)
     for c in twin_in:
@@ -313,24 +312,26 @@
             device_id=along_z(o), device_id_type=MESH,
         )
 
+    way = 1 - 2 * core
     score(4, 0)
 
     def two(i, carry):
+        a, b = 4 + way * i, 4 - way * (i + 1)
         peak = peaks[0]
-        score(3 - i, 1)
-        weigh(4 + i, 0, peak)
-        home_copy(4 + i).start()
+        score(b, 1)
+        weigh(a, 0, peak)
+        home_copy(a).start()
         peak = peaks[1]
-        score(5 + i, 0)
-        weigh(3 - i, 1, peak)
-        home_copy(3 - i).start()
+        score(a + way, 0)
+        weigh(b, 1, peak)
+        home_copy(b).start()
         return carry
 
     lax.fori_loop(0, 3, two, 0)
     peak = peaks[0]
     score(0, 1)
-    weigh(7, 0, peak)
-    home_copy(7).start()
+    weigh(4 + 3 * way, 0, peak)
+    home_copy(4 + 3 * way).start()
     weigh(0, 1, peaks[1])
     o_all[z] = o_send[0]
     for o in far_first:

time: 49.1 us -> 49 us (level)
  no operation moved by 1% of the time
where the time goes in v5:
time: 49 us; the launch traced here: 48.9 us
  Pallas kernels  48.1 us (98%)
  local copies, waits for them, and re-layouts  0.8 us (2%)
    pallas_call x1, Pallas kernels, shards(): pl.pallas_call(kernel, out_shape=pltpu.VMEM(queries.shape, bf), in_specs=...  48.1 us

profile of v5, /device:TPU:1, one launch (start us, length us, event | category | flops | bytes accessed | tf_op | source)
XLA Modules:
  0.0 48.9 jit_solution(8454253368542411906)
XLA Ops:
  0.0 48.1 %attend.1 = bf16[32,64,128]{2,1,0:T(8,128)(2,1)S(1)} custom-call(s32[64,128]{1,0:T(8,128)} %bitcast.1, s32[16]{0:T(128)} %docs_hbm.1, bf16[32,64,128]{2,1,0:T(8,128)(2,1)} %q_hbm.1, bf16[32,8,128]{2,1,0:T(8,128)(2,1)} %k_hbm.1, bf16[32,8,128]{2,1,0:T(8,128)(2,1)} %v_hbm.1, s32[32,8,128]{2,1,0:T(8,128)} %off_hbm.1, s32[8,128]{1,0:T(8,128)} %smooth_hbm.1, ...), custom_call_target="tpu_custom_call" | custom-call | tf_op jit(solution)/shard_map/attend/pallas_call | solution.py:355
  48.1 0.8 %copy.10 = bf16[32,64,128]{2,1,0:T(8,128)(2,1)} copy(bf16[32,64,128]{2,1,0:T(8,128)(2,1)S(1)} %attend.1) | data formatting | bytes 1048576

commit v6 on v4

--- a/solution.py
+++ b/solution.py
@@ -18,6 +18,7 @@
 SORTED = REACH + BLOCKS + 8
 DOCS = 16
 BIG = 65536.0
+HALF = N_ROWS // 2
 FACTOR = DIM**-0.5 * 1.4426950408889634
 LOW = -1e30
 
@@ -276,9 +277,10 @@
         blocks = ref[pl.ds(block_at(o) + c0 // TOK, width // TOK)]
         return blocks.reshape(width, 2 * DIM)
 
-    def score(o, slot):
-        q = jnp.concatenate([q_all[o], q_doc[o]], axis=1)
-        top = jnp.full((N_ROWS, DIM), LOW, jnp.float32)
+    def score(o, slot, first=0, n=N_ROWS):
+        part = slice(first, first + n)
+        q = jnp.concatenate([q_all[o, part], q_doc[o, part]], axis=1)
+        top = jnp.full((n, DIM), LOW, jnp.float32)
         for c0 in range(0, PAD, CHUNK):
             width = min(CHUNK, PAD - c0)
             s = lax.dot_general(
@@ -288,24 +290,24 @@
             for t in range(0, width, DIM):
                 tile = s[:, t : t + DIM]
                 if c0 + t == REACH * TOK:
-                    tile = jnp.where(causal, tile, LOW)
-                scores[slot, :, c0 + t : c0 + t + DIM] = tile
+                    tile = jnp.where(causal[part], tile, LOW)
+                scores[slot, :n, c0 + t : c0 + t + DIM] = tile
                 top = jnp.maximum(top, tile)
-        peaks[slot] = jnp.broadcast_to(jnp.max(top, axis=1, keepdims=True), (N_ROWS, DIM))
-
-    def weigh(o, slot, peak):
-        total = jnp.zeros((N_ROWS, 2 * DIM), jnp.float32)
+        peaks[slot, :n] = jnp.broadcast_to(jnp.max(top, axis=1, keepdims=True), (n, DIM))
+
+    def weigh(o, slot, peak, first=0, n=N_ROWS):
+        total = jnp.zeros((n, 2 * DIM), jnp.float32)
         for c0 in range(0, PAD, CHUNK):
             width = min(CHUNK, PAD - c0)
             tiles = [
-                jnp.exp2((scores[slot, :, c0 + t : c0 + t + DIM] - peak) * FACTOR)
+                jnp.exp2((scores[slot, :n, c0 + t : c0 + t + DIM] - peak) * FACTOR)
                 for t in range(0, width, DIM)
             ]
             w = jnp.concatenate([tile.astype(jnp.bfloat16) for tile in tiles], axis=1)
             total = total + jnp.dot(
                 w, window(vals, o, c0, width), preferred_element_type=jnp.float32
             )
-        o_send[o] = (total[:, :DIM] / total[:, DIM:]).astype(jnp.bfloat16)
+        o_send[o, first : first + n] = (total[:, :DIM] / total[:, DIM:]).astype(jnp.bfloat16)
 
     def home_copy(o):
         return pltpu.make_async_remote_copy(
@@ -313,28 +315,44 @@
             device_id=along_z(o), device_id_type=MESH,
         )
 
-    score(4, 0)
+    def half_copy(o, h):
+        part = pl.ds(h * HALF, HALF)
+        return pltpu.make_async_remote_copy(
+            o_send.at[o, part], o_all.at[z, part], os.at[o + 8 * h], orr.at[8 - o + 8 * h],
+            device_id=along_z(o), device_id_type=MESH,
+        )
+
+    split = (4, 3)
+    halves = [(o, h) for o in split for h in range(2)]
+    score(halves[0][0], 0, 0, HALF)
+    for n, (o, h) in enumerate(halves):
+        peak = peaks[n % 2, :HALF]
+        if n + 1 < len(halves):
+            score(halves[n + 1][0], 1 - n % 2, halves[n + 1][1] * HALF, HALF)
+        else:
+            score(5, 0)
+        weigh(o, n % 2, peak, h * HALF, HALF)
+        half_copy(o, h).start()
 
     def two(i, carry):
         peak = peaks[0]
-        score(3 - i, 1)
-        weigh(4 + i, 0, peak)
-        home_copy(4 + i).start()
+        score(2 - i, 1)
+        weigh(5 + i, 0, peak)
+        home_copy(5 + i).start()
         peak = peaks[1]
-        score(5 + i, 0)
-        weigh(3 - i, 1, peak)
-        home_copy(3 - i).start()
+        score(jnp.minimum(6 + i, 7), 0)
+        weigh(2 - i, 1, peak)
+        pl.when(i < 2)(home_copy(2 - i).start)
         return carry
 
     lax.fori_loop(0, 3, two, 0)
-    peak = peaks[0]
-    score(0, 1)
-    weigh(7, 0, peak)
-    home_copy(7).start()
-    weigh(0, 1, peaks[1])
     o_all[z] = o_send[0]
     for o in far_first:
-        home_copy(o).wait_recv()
+        if o in split:
+            half_copy(o, 0).wait_recv()
+            half_copy(o, 1).wait_recv()
+        else:
+            home_copy(o).wait_recv()
     for g in range(HEADS // 2):
         pair = [
             o_all[2 * g + i].astype(jnp.float32).reshape(TOK, GROUP, DIM) for i in range(2)
@@ -344,7 +362,11 @@
     for c in list(kv_copies.values()) + q_copies + sends:
         c.wait_send()
     for o in far_first:
-        home_copy(o).wait_send()
+        if o in split:
+            half_copy(o, 0).wait_send()
+            half_copy(o, 1).wait_send()
+        else:
+            home_copy(o).wait_send()
 
 
 def shards(queries, keys, values, offsets, smooth_exp, scale_exp, placement, doc_lengths):
@@ -380,7 +402,7 @@
             pltpu.VMEM((SORTED, TOK, 2 * DIM), bf),
             pltpu.VMEM((2, N_ROWS, PAD), f32),
             pltpu.VMEM((2, N_ROWS, DIM), f32),
-            dma((8,)), dma((4, 2)), dma((8,)), dma((8,)), dma((8,)), dma((8,)),
+            dma((8,)), dma((4, 2)), dma((8,)), dma((8,)), dma((16,)), dma((16,)),
             dma((60,)), dma((60,)), dma((10,)),
         ],
         compiler_params=pltpu.CompilerParams(

time: 49.1 us -> 48.9 us (level)
  no operation moved by 1% of the time
where the time goes in v6:
time: 48.9 us; the launch traced here: 48.8 us
  Pallas kernels  48 us (98%)
  local copies, waits for them, and re-layouts  0.8 us (2%)
    pallas_call x1, Pallas kernels, shards(): pl.pallas_call(kernel, out_shape=pltpu.VMEM(queries.shape, bf), in_specs=...  48 us

profile of v6, /device:TPU:1, one launch (start us, length us, event | category | flops | bytes accessed | tf_op | source)
XLA Modules:
  0.0 48.8 jit_solution(9690373028351843572)
XLA Ops:
  0.0 48.0 %attend.1 = bf16[32,64,128]{2,1,0:T(8,128)(2,1)S(1)} custom-call(s32[64,128]{1,0:T(8,128)} %bitcast.1, s32[16]{0:T(128)} %docs_hbm.1, bf16[32,64,128]{2,1,0:T(8,128)(2,1)} %q_hbm.1, bf16[32,8,128]{2,1,0:T(8,128)(2,1)} %k_hbm.1, bf16[32,8,128]{2,1,0:T(8,128)(2,1)} %v_hbm.1, s32[32,8,128]{2,1,0:T(8,128)} %off_hbm.1, s32[8,128]{1,0:T(8,128)} %smooth_hbm.1, ...), custom_call_target="tpu_custom_call" | custom-call | tf_op jit(solution)/shard_map/attend/pallas_call | solution.py:376
  48.0 0.8 %copy.10 = bf16[32,64,128]{2,1,0:T(8,128)(2,1)} copy(bf16[32,64,128]{2,1,0:T(8,128)(2,1)S(1)} %attend.1) | data formatting | bytes 1048576
